TPU v7x, 512 devices: a whole 4x4x16 slice. The times are simulated.
512 devices in a mesh: leaf: 128 (over y_hi, z, x), sub: 4 (over y_lo, core).
Axes of the slice: x: 4, y: 4 (y_hi: 2, y_lo: 2; y = y_hi * 2 + y_lo), z: 16, core: 2. Of those that a mesh axis runs over, the one named last changes fastest.
Arguments:
- x_user: float32 [16, 1048576], P(None, ('leaf', 'sub')), may hold values from -6 to 6
- morton_order: int32 [512, 2048], P(('leaf', 'sub')), may hold values from 0 to 2047, each once within a row
- points: float32 [3, 1048576], P(None, ('leaf', 'sub')), may hold values from -1 to 1
- leaf_basis: float32 [16384, 4096], P(('leaf', 'sub')), may hold values from -0.75 to 0.75
- near_list: int32 [16384, 27], P(('leaf', 'sub')), may hold values from 0 to 16383, as said below
- far_leaf: int32 [16384, 24], P(('leaf', 'sub')), may hold values from 0 to 16383, as said below
- leaf_skeleton: float32 [16384, 192], P(('leaf', 'sub')), may hold values from -1 to 1
- leaf_transfer: float32 [16384, 4096], P(('leaf', 'sub')), may hold values from -0.25 to 0.25
- leaf_parent: int32 [16384], P(('leaf', 'sub')), may hold values from 0 to 2047, as said below
- cluster_skeleton: float32 [2048, 192], P('leaf'), may hold values from -1 to 1
- far_cluster: int32 [2048, 16], P('leaf'), may hold values from 0 to 2047, as said below
- cluster_transfer: float32 [2048, 4096], P('leaf'), may hold values from -0.25 to 0.25
- cluster_parent: int32 [2048], P('leaf'), may hold values from 0 to 511, as said below
- top_skeleton: float32 [512, 192], P('leaf'), may hold values from -1 to 1
- far_top: int32 [512, 128], replicated, may hold values from 0 to 511
- top_counts: int32 [512], replicated, may hold values from 1 to 128, 8192 in all
Outputs:
- product: float32 [16, 1048576], P(None, ('leaf', 'sub'))
Inputs may be any that keep to these rules, and one draw needn't show every extreme that they name: `near_list`: entry 0 of row i is leaf i itself; every other entry is a leaf 1 to 16 positions from i in Morton order. `far_leaf`: every entry of row i is a leaf more than 16 and at most 32 positions from i in Morton order. `leaf_parent`: never falls; leaf i with g = i // 128 has a parent from g * 16 to g * 16 + 15, and each level-1 cluster has at least one leaf. `far_cluster`: every entry of row c is a level-1 cluster 1 to 12 positions from c. `cluster_parent`: never falls; cluster c with g = c // 16 has a parent from g * 4 to g * 4 + 3, and each top-level cluster has at least one child. `top_counts`: the counts sum to 8192; slots of far_top beyond a row's count are not used.
All inputs are finite; a program needn't handle non-finite values.
Results may differ from a plain program's by a relative error of at most 0.00011.
Values sent between devices are 32-bit elements; how exact they have to be, the bound alone decides.
No kernel may reach another device: no remote copies, remote signals or barrier semaphores. Data moves between devices by JAX's collectives and lax.ppermute only.
A program may use at most 64 MiB of HBM per device.

v0:
```python
import functools

import jax
import jax.numpy as jnp
from jax import lax
from jax.experimental import pallas as pl
from jax.experimental.pallas import tpu as pltpu
from jax.sharding import PartitionSpec as P

COLS = 16
LEAF = 64
RANK = 64
NB = 27
RN = 16
RF = 32
F0 = 24
F1 = 16
C2 = 4
MAXF2 = 128
LD = 32
C1 = 16
SUB = 4
PTS = LD * LEAF
TILE = 128
ROWS = 40

INV_FOUR_PI = 0.07957747154594767
SOFTENING = 0.0025
F32 = jnp.float32
BF16 = jnp.bfloat16
VMEM_LIMIT = 48 * 1024 * 1024


def split(value):
    high = value.astype(BF16)
    low = (value - high.astype(F32)).astype(BF16)
    return high, low


def small_dot(lhs, rhs, transposed=False):
    dims = (((1,), (1,)), ((), ())) if transposed else (((1,), (0,)), ((), ()))
    rows = lhs.shape[0]
    lhs_high, lhs_low = split(lhs)
    rhs_high, rhs_low = split(rhs)
    both = jnp.concatenate([lhs_high, lhs_low], axis=0)
    first = lax.dot_general(both, rhs_high, dims, preferred_element_type=F32)
    second = lax.dot_general(lhs_high, rhs_low, dims, preferred_element_type=F32)
    return first[:rows] + first[rows:] + second


def permuted(read, index_rows, write):
    for out_tile in range(PTS // TILE):
        index = jnp.broadcast_to(index_rows(out_tile), (8, TILE))
        lane = index & (TILE - 1)
        source = index >> 7
        for half in range(2):
            total = jnp.zeros((8, TILE), F32)
            for tile in range(PTS // TILE):
                picked = jnp.take_along_axis(read(half, tile), lane, axis=1, mode="promise_in_bounds")
                total = jnp.where(source == tile, picked, total)
            write(half, out_tile, total)


def to_tile(value):
    return jnp.concatenate([value[:8], value[8:]], axis=1)


def from_tile(tile):
    return jnp.concatenate([tile[:, :RANK], tile[:, RANK:]], axis=0)


def upward_kernel(
    leaf_slot, cluster_slot, x_ref, order_ref, points_ref, skel_ref, basis_ref, transfer_ref,
    cluster_transfer_ref, pay_ref, s1_ref, s2_ref, s1_acc, s2_acc,
):
    def read(half, tile):
        return x_ref[half * 8 : half * 8 + 8, tile * TILE : (tile + 1) * TILE]

    def write(half, tile, value):
        pay_ref[half * 8 : half * 8 + 8, tile * TILE : (tile + 1) * TILE] = value

    permuted(read, lambda tile: order_ref[:, tile * TILE : (tile + 1) * TILE], write)
    pay_ref[32:35, :] = points_ref[...]
    pay_ref[35:38, :] = skel_ref[...]
    pay_ref[38:40, :] = jnp.zeros((2, PTS), F32)
    s1_acc[...] = jnp.zeros_like(s1_acc)
    s2_acc[...] = jnp.zeros_like(s2_acc)
    for leaf in range(LD):
        values = pay_ref[:16, leaf * LEAF : (leaf + 1) * LEAF]
        coef = small_dot(values, basis_ref[leaf])
        pay_ref[16:32, leaf * LEAF : (leaf + 1) * LEAF] = coef
        slot = leaf_slot[leaf]
        s1_acc[slot] = s1_acc[slot] + small_dot(coef, transfer_ref[leaf])
    for cluster in range(C1):
        coef = s1_acc[cluster]
        s1_ref[cluster * 8 : cluster * 8 + 8, :] = to_tile(coef)
        slot = cluster_slot[cluster]
        s2_acc[slot] = s2_acc[slot] + small_dot(coef, cluster_transfer_ref[cluster])
    for top in range(C2):
        s2_ref[top * 8 : top * 8 + 8, :] = to_tile(s2_acc[top])


def source_pair(first, second):
    lane = lax.broadcasted_iota(jnp.int32, (8, TILE), 1)
    return jnp.where(lane < RANK, first, second)


def green(target, source):
    dx = target[0] - source[0:1]
    dy = target[1] - source[1:2]
    dz = target[2] - source[2:3]
    return lax.rsqrt(dx * dx + dy * dy + dz * dz + SOFTENING)


def spread(columns):
    return [jnp.broadcast_to(columns[:, k : k + 1], (LEAF, TILE)) for k in range(3)]


def quad_product(target, sources, weights):
    high, low = [], []
    for first, second in ((0, 1), (2, 3)):
        block = green(target, source_pair(sources[first], sources[second]))
        block_high, block_low = split(block)
        high.append(block_high)
        low.append(block_low)
    lhs = jnp.concatenate(
        [jnp.concatenate(high, axis=1), jnp.concatenate(low, axis=1)], axis=0
    )
    rhs = jnp.concatenate(weights, axis=0)
    return jnp.dot(lhs, rhs, preferred_element_type=F32)


def listed_product(target, indices, place_ref, weight_ref):
    total = None
    for quad in range(len(indices) // 4):
        group = indices[quad * 4 : quad * 4 + 4]
        part = quad_product(target, [place_ref[i] for i in group], [weight_ref[i] for i in group])
        total = part if total is None else total + part
    return total[:LEAF] + total[LEAF:]


def weights_of(values):
    high = values.astype(BF16).astype(F32)
    low = values - high
    return jnp.concatenate([high, low], axis=0).T.astype(BF16)


def stage_pair(pay, row_value, row_place, tile, place_ref, weight_ref, slot):
    lanes = slice(tile * TILE, (tile + 1) * TILE)
    weights = weights_of(pay[row_value : row_value + 16, lanes])
    weight_ref[slot] = weights[:LEAF]
    weight_ref[slot + 1] = weights[LEAF:]
    place = pay[row_place : row_place + 3, lanes]
    swapped = pltpu.roll(place, RANK, 1)
    lane = lax.broadcasted_iota(jnp.int32, (3, TILE), 1)
    place_ref[slot, 0:3] = jnp.where(lane < RANK, place, swapped)
    place_ref[slot + 1, 0:3] = jnp.where(lane < RANK, swapped, place)


def finish_rows(result_ref, count, write):
    for pair in range(count // 2):
        block = result_ref[pair * TILE : (pair + 1) * TILE, :].T
        write(pair, (block[:16] + block[16:]) * INV_FOUR_PI)


def interaction_kernel(
    near_ids, far_ids, cluster_ids, sub_pos, order_ref, before_ref, own_ref, after_ref,
    cl_before_ref, cl_own_ref, cl_after_ref,
    near_ref, far_ref, z1_ref, inverse_ref,
    near_place, near_weight, far_place, far_weight, cl_place, cl_weight, target_cols,
    near_rows, far_rows, cl_rows,
):
    tiles = PTS // TILE
    for tile in range(tiles // 2):
        stage_pair(before_ref, 0, 32, tiles // 2 + tile, near_place, near_weight, 2 * tile)
        stage_pair(after_ref, 0, 32, tile, near_place, near_weight, RN + LD + 2 * tile)
    for tile in range(tiles):
        stage_pair(own_ref, 0, 32, tile, near_place, near_weight, RN + 2 * tile)
        stage_pair(before_ref, 16, 35, tile, far_place, far_weight, 2 * tile)
        stage_pair(own_ref, 16, 35, tile, far_place, far_weight, LD + 2 * tile)
        stage_pair(after_ref, 16, 35, tile, far_place, far_weight, 2 * LD + 2 * tile)
    near_weight[2 * RN + LD] = jnp.zeros((LEAF, 32), BF16)
    near_place[2 * RN + LD, 0:3] = jnp.zeros((3, TILE), F32)
    for part, ref in enumerate((cl_before_ref, cl_own_ref, cl_after_ref)):
        for cluster in range(C1):
            slot = part * C1 + cluster
            tile = ref[cluster * 8 : cluster * 8 + 8, :]
            cl_weight[slot] = weights_of(from_tile(tile))
        for pair in range(C1 // 2):
            slot = part * C1 + 2 * pair
            place = jnp.concatenate(
                [ref[TILE + 8 * k + pair : TILE + 8 * k + pair + 1, :] for k in range(3)], axis=0
            )
            swapped = pltpu.roll(place, RANK, 1)
            lane = lax.broadcasted_iota(jnp.int32, (3, TILE), 1)
            cl_place[slot, 0:3] = jnp.where(lane < RANK, place, swapped)
            cl_place[slot + 1, 0:3] = jnp.where(lane < RANK, swapped, place)
    for tile in range(tiles):
        block = own_ref[32:40, tile * TILE : (tile + 1) * TILE].T
        target_cols[2 * tile] = block[:LEAF]
        target_cols[2 * tile + 1] = block[LEAF:]

    def leaf_step(leaf, carry):
        columns = target_cols[leaf]
        target = spread(columns)
        ids = [near_ids[leaf * NB + k] for k in range(NB)] + [2 * RN + LD]
        near_rows[pl.ds(leaf * LEAF, LEAF), :] = listed_product(target, ids, near_place, near_weight)
        target = spread(columns[:, 3:6])
        ids = [far_ids[leaf * F0 + k] for k in range(F0)]
        far_rows[pl.ds(leaf * LEAF, LEAF), :] = listed_product(target, ids, far_place, far_weight)
        return carry

    lax.fori_loop(0, LD, leaf_step, 0)

    def cluster_step(k, carry):
        mine = sub_pos[0] * (C1 // SUB) + k
        columns = cl_place[C1 + mine].T
        target = spread(columns[:LEAF])
        ids = [cluster_ids[mine * F1 + j] for j in range(F1)]
        cl_rows[pl.ds(k * LEAF, LEAF), :] = listed_product(target, ids, cl_place, cl_weight)
        return carry

    lax.fori_loop(0, C1 // SUB, cluster_step, 0)

    def write_near(pair, block):
        near_ref[:, pair * TILE : (pair + 1) * TILE] = block

    def write_far(pair, block):
        far_ref[:, pair * TILE : (pair + 1) * TILE] = block

    def write_cluster(pair, block):
        z1_ref[pair * 16 : pair * 16 + 8, :] = to_tile(block[:, :RANK])
        z1_ref[pair * 16 + 8 : pair * 16 + 16, :] = to_tile(block[:, RANK:])

    finish_rows(near_rows, LD, write_near)
    finish_rows(far_rows, LD, write_far)
    finish_rows(cl_rows, C1 // SUB, write_cluster)

    order = order_ref[...]
    position = lax.broadcasted_iota(jnp.int32, (16, PTS), 1)
    hit = (order >> 7) == lax.broadcasted_iota(jnp.int32, (16, PTS), 0)
    coarse = jnp.where(hit, (position >> 7).astype(F32), 0.0)
    fine = jnp.where(hit, (position & (TILE - 1)).astype(F32), 0.0)
    lhs = jnp.concatenate([coarse, fine], axis=0).astype(BF16)
    lane_of = (order & (TILE - 1)) == lax.broadcasted_iota(jnp.int32, (TILE, PTS), 0)
    rhs = jnp.where(lane_of, 1.0, 0.0).astype(BF16)
    found = lax.dot_general(lhs, rhs, (((1,), (1,)), ((), ())), preferred_element_type=F32)
    inverse_ref[...] = found[:16].astype(jnp.int32) * TILE + found[16:].astype(jnp.int32)


def top_kernel(lists, counts, source_ref, target_ref, z1_ref, out_ref, rows):
    for top in range(C2):
        skel = target_ref[top]
        target = spread(skel.T[:LEAF])
        rows[top * LEAF : (top + 1) * LEAF, :] = jnp.zeros((LEAF, 32), F32)

        def step(pair, carry, top=top, target=target):
            places, weights = [], []
            for k in range(2):
                at = 2 * pair + k
                source = lists[top * MAXF2 + at]
                live = jnp.where(at < counts[top], 1.0, 0.0).astype(F32)
                tile = jnp.concatenate(
                    [source_ref[source, :, j * TILE : (j + 1) * TILE] for j in range(8)], axis=0
                )
                weights.append(weights_of(from_tile(tile) * live))
                first = source_ref[source, :, 8 * TILE : 9 * TILE]
                second = source_ref[source, :, 9 * TILE : 10 * TILE]
                places.append((first, second))
            (a0, a1), (b0, b1) = places
            lane = lax.broadcasted_iota(jnp.int32, (1, TILE), 1)
            xs = jnp.where(lane < RANK, a0, pltpu.roll(b0, RANK, 1))
            ys = jnp.where(lane < RANK, pltpu.roll(a0, RANK, 1), b0)
            zs = jnp.where(lane < RANK, a1, pltpu.roll(b1, RANK, 1))
            block = lax.rsqrt(
                (target[0] - xs) * (target[0] - xs)
                + (target[1] - ys) * (target[1] - ys)
                + (target[2] - zs) * (target[2] - zs)
                + SOFTENING
            )
            high, low = split(block)
            part = jnp.dot(
                jnp.concatenate([high, low], axis=0),
                jnp.concatenate(weights, axis=0),
                preferred_element_type=F32,
            )
            where = slice(top * LEAF, (top + 1) * LEAF)
            rows[where, :] = rows[where, :] + part[:LEAF] + part[LEAF:]
            return carry

        lax.fori_loop(0, (counts[top] + 1) // 2, step, 0)

    def write(pair, block):
        out_ref[pair * 16 : pair * 16 + 8, :] = to_tile(block[:, :RANK])
        out_ref[pair * 16 + 8 : pair * 16 + 16, :] = to_tile(block[:, RANK:])

    finish_rows(rows, C2, write)
    out_ref[C2 * 8 :, :] = z1_ref[...]


def downward_kernel(
    leaf_slot, cluster_slot, group_ref, near_ref, far_ref, inverse_ref, basis_ref, transfer_ref,
    cluster_transfer_ref, out_ref, z2_acc, w1_acc, morton,
):
    for top in range(C2):
        tile = group_ref[0, top * 8 : top * 8 + 8, :]
        for part in range(1, SUB):
            tile = tile + group_ref[part, top * 8 : top * 8 + 8, :]
        z2_acc[top] = from_tile(tile)
    for cluster in range(C1):
        part, place = divmod(cluster, C1 // SUB)
        at = C2 * 8 + place * 8
        local = from_tile(group_ref[part, at : at + 8, :])
        w1_acc[cluster] = local + small_dot(
            z2_acc[cluster_slot[cluster]], cluster_transfer_ref[cluster], True
        )
    for leaf in range(LD):
        lanes = slice(leaf * LEAF, (leaf + 1) * LEAF)
        local = far_ref[:, lanes] + small_dot(w1_acc[leaf_slot[leaf]], transfer_ref[leaf], True)
        morton[:, lanes] = near_ref[:, lanes] + small_dot(local, basis_ref[leaf], True)

    def read(half, tile):
        return morton[half * 8 : half * 8 + 8, tile * TILE : (tile + 1) * TILE]

    def write(half, tile, value):
        out_ref[half * 8 : half * 8 + 8, tile * TILE : (tile + 1) * TILE] = value

    permuted(read, lambda tile: inverse_ref[tile : tile + 1, :], write)


SMEM = pl.BlockSpec(memory_space=pltpu.SMEM)
VMEM = pl.BlockSpec(memory_space=pltpu.VMEM)


def call(body, scalars, arrays, outs, scratch, flops=0, trans=0):
    return pl.pallas_call(
        body,
        in_specs=[SMEM] * len(scalars) + [VMEM] * len(arrays),
        out_specs=[VMEM] * len(outs),
        out_shape=[jax.ShapeDtypeStruct(shape, dtype) for shape, dtype in outs],
        scratch_shapes=scratch,
        compiler_params=pltpu.CompilerParams(vmem_limit_bytes=VMEM_LIMIT),
        cost_estimate=pl.CostEstimate(flops=flops, bytes_accessed=4 * 1024 * 1024, transcendentals=trans),
    )(*scalars, *arrays)


def linear_shift(value, step):
    size = lax.axis_size("leaf") * lax.axis_size("sub")
    pairs = [(i, i + step) for i in range(size) if 0 <= i + step < size]
    return lax.ppermute(value, ("leaf", "sub"), pairs)


def leaf_shift(value, step):
    size = lax.axis_size("leaf")
    pairs = [(i, i + step) for i in range(size) if 0 <= i + step < size]
    return lax.ppermute(value, "leaf", pairs)


def local(
    x_user, morton_order, points, leaf_basis, near_list, far_leaf, leaf_skeleton, leaf_transfer,
    leaf_parent, cluster_skeleton, far_cluster, cluster_transfer, cluster_parent, top_skeleton,
    far_top, top_counts,
):
    leaf_count = lax.axis_size("leaf")
    leaf_pos = lax.axis_index("leaf")
    sub_pos = lax.axis_index("sub")
    first_leaf = (leaf_pos * SUB + sub_pos) * LD
    basis = leaf_basis.reshape(LD, LEAF, RANK)
    transfer = leaf_transfer.reshape(LD, RANK, RANK)
    cluster_trans = cluster_transfer.reshape(C1, RANK, RANK)
    skel_rows = leaf_skeleton.reshape(LD, 3, RANK).transpose(1, 0, 2).reshape(3, PTS)
    leaf_slot = leaf_parent - leaf_pos * C1
    cluster_slot = cluster_parent - leaf_pos * C2

    pay, s1_part, s2_part = call(
        upward_kernel,
        [leaf_slot, cluster_slot],
        [x_user, morton_order, points, skel_rows, basis, transfer, cluster_trans],
        [((ROWS, PTS), F32), ((C1 * 8, TILE), F32), ((C2 * 8, TILE), F32)],
        [pltpu.VMEM((C1, COLS, RANK), F32), pltpu.VMEM((C2, COLS, RANK), F32)],
    )

    s2 = lax.all_to_all(s2_part.reshape(SUB, 8, TILE), "sub", 0, 0).sum(axis=0)
    top_row = lax.dynamic_index_in_dim(top_skeleton, sub_pos, 0, keepdims=True)
    top_load = jnp.concatenate([s2.reshape(1, 8 * TILE), top_row, jnp.zeros((1, RANK), F32)], axis=1)
    top_all = lax.all_to_all(
        jnp.broadcast_to(top_load[None], (leaf_count, 1, 10 * TILE)), "leaf", 0, 0, tiled=True
    )

    before = linear_shift(pay, 1)
    after = linear_shift(pay, -1)
    s1 = lax.all_to_all(jnp.broadcast_to(s1_part, (SUB, C1 * 8, TILE)), "sub", 0, 0).sum(axis=0)
    cl_skel = cluster_skeleton.reshape(C1, 3, RANK).transpose(1, 0, 2).reshape(24, TILE)
    cl_own = jnp.concatenate([s1, cl_skel], axis=0)
    cl_before = leaf_shift(cl_own, 1)
    cl_after = leaf_shift(cl_own, -1)

    near_ids = (near_list - first_leaf + RN).reshape(-1)
    far_ids = (far_leaf - first_leaf + RF).reshape(-1)
    cluster_ids = (far_cluster - (leaf_pos - 1) * C1).reshape(-1)
    near_sum, far_sum, z1, inverse = call(
        interaction_kernel,
        [near_ids, far_ids, cluster_ids, sub_pos.reshape(1)],
        [morton_order, before, pay, after, cl_before, cl_own, cl_after],
        [
            ((COLS, PTS), F32),
            ((COLS, PTS), F32),
            ((C1 // SUB * 8, TILE), F32),
            ((16, TILE), jnp.int32),
        ],
        [
            pltpu.VMEM((2 * RN + LD + 1, 8, TILE), F32),
            pltpu.VMEM((2 * RN + LD + 1, LEAF, 32), BF16),
            pltpu.VMEM((3 * LD, 8, TILE), F32),
            pltpu.VMEM((3 * LD, LEAF, 32), BF16),
            pltpu.VMEM((3 * C1, 8, TILE), F32),
            pltpu.VMEM((3 * C1, LEAF, 32), BF16),
            pltpu.VMEM((LD, LEAF, 8), F32),
            pltpu.VMEM((PTS, 32), F32),
            pltpu.VMEM((PTS, 32), F32),
            pltpu.VMEM((C1 // SUB * LEAF, 32), F32),
        ],
        flops=20 * 7_000_000,
        trans=7_000_000,
    )

    top_first = leaf_pos * C2
    my_top = lax.dynamic_slice_in_dim(far_top, top_first, C2, 0)
    my_counts = lax.dynamic_slice_in_dim(top_counts, top_first, C2, 0)
    slots = jnp.arange(MAXF2, dtype=jnp.int32)
    wanted = (slots[None, :] < my_counts[:, None]) & (my_top % SUB == sub_pos)
    rank_of = jnp.sum(
        (wanted[:, None, :] & (slots[None, None, :] < slots[None, :, None])).astype(jnp.int32), axis=2
    )
    chosen = wanted[:, :, None] & (rank_of[:, :, None] == slots[None, None, :])
    lists = jnp.sum(jnp.where(chosen, (my_top // SUB)[:, :, None], 0), axis=1).reshape(-1)
    counts = jnp.sum(wanted.astype(jnp.int32), axis=1)
    target_skel = jnp.pad(top_skeleton.reshape(C2, 3, RANK), ((0, 0), (0, 5), (0, TILE - RANK)))
    (share,) = call(
        top_kernel,
        [lists, counts],
        [top_all, target_skel, z1],
        [(((C2 + C1 // SUB) * 8, TILE), F32)],
        [pltpu.VMEM((C2 * LEAF, 32), F32)],
    )
    group = lax.all_to_all(
        jnp.broadcast_to(share, (SUB, (C2 + C1 // SUB) * 8, TILE)), "sub", 0, 0
    )
    (product,) = call(
        downward_kernel,
        [leaf_slot, cluster_slot],
        [group, near_sum, far_sum, inverse, basis, transfer, cluster_trans],
        [((COLS, PTS), F32)],
        [
            pltpu.VMEM((C2, COLS, RANK), F32),
            pltpu.VMEM((C1, COLS, RANK), F32),
            pltpu.VMEM((COLS, PTS), F32),
        ],
    )
    return product


def solution(mesh):
    both = ("leaf", "sub")
    placed = (
        P(None, both), P(both, None), P(None, both), P(both, None), P(both, None), P(both, None),
        P(both, None), P(both, None), P(both), P("leaf", None), P("leaf", None), P("leaf", None),
        P("leaf"), P("leaf", None), P(), P(),
    )
    return jax.shard_map(
        local, mesh=mesh, in_specs=placed, out_specs=P(None, both), check_vma=False
    )
```

profile of v0, /device:TPU:118, one launch (start us, length us, event | category | flops | bytes accessed | tf_op | source)
XLA Modules:
  0.0 141.9 jit_solution(13261413354208438294)
XLA Ops:
  0.0 1.5 %reshape.71.basis_ref = f32[32,64,64]{2,1,0:T(8,128)S(1)} reshape(f32[32,4096]{1,0:T(8,128)} %param.19) | data formatting | bytes 1048576 | tf_op jit(solution)/shard_map/reshape | solution.py:368
  5.2 5.3 %shard_map.154 = (f32[40,2048]{1,0:T(8,128)S(1)}, f32[128,128]{1,0:T(8,128)S(1)}, f32[32,128]{1,0:T(8,128)S(1)}) custom-call(s32[32]{0:T(128)S(1)} %broadcast_subtract_fusion.2.leaf_slot, s32[16]{0:T(128)S(1)} %broadcast_subtract_fusion.1.cluster_slot, f32[16,2048]{1,0:T(8,128)S(1)} %copy-done, s32[1,2048]{1,0:T(1,128)S(1)} %copy-done.4, ...), custom_call_target="tpu_custom_call" | custom-call | bytes 4194304 | tf_op jit(solution)/shard_map/pallas_call | solution.py:336
  11.2 6.2 %all_to_all.20 = f32[4,8,128]{2,1,0:T(8,128)S(1)} all-to-all(f32[4,8,128]{2,1,0:T(8,128)S(1)} %bitcast.6), channel_id=1, replica_groups=mesh['leaf'=128,'sub'=4] {'sub'}, dimensions={0} | all-to-all | bytes 32768 | tf_op jit(solution)/shard_map/all_to_all | solution.py:383
  18.1 3.4 %all-to-all-start.2 = ((f32[4,128,128]{2,1,0:T(8,128)}), f32[4,128,128]{2,1,0:T(8,128)S(1)}, u32[]{:S(2)}, u32[]{:S(2)}) async-start(f32[4,128,128]{2,1,0:T(8,128)} %broadcast_in_dim.43), calls=%async_computation.2 | async-start | bytes 524288 | tf_op jit(solution)/shard_map/all_to_all | solution.py:392
  22.3 5.2 %all-to-all-done.2 = f32[4,128,128]{2,1,0:T(8,128)S(1)} async-done(((f32[4,128,128]{2,1,0:T(8,128)}), f32[4,128,128]{2,1,0:T(8,128)S(1)}, u32[]{:S(2)}, u32[]{:S(2)}) %all-to-all-start.2) | async-done | bytes 262176 | tf_op jit(solution)/shard_map/all_to_all | solution.py:392
  27.5 1.2 broadcast_in_dim.42
  28.7 20.8 %all-to-all-start.1 = ((f32[128,1,1280]{2,1,0:T(1,128)}), f32[128,1,1280]{2,1,0:T(1,128)S(1)}, u32[]{:S(2)}, u32[]{:S(2)}) async-start(f32[128,1,1280]{2,1,0:T(1,128)} %broadcast_in_dim.42), calls=%async_computation.1 | async-start | bytes 1310720 | tf_op jit(solution)/shard_map/all_to_all | solution.py:386
  49.6 1.9 %collective-permute-start = (f32[40,2048]{1,0:T(8,128)}, f32[40,2048]{1,0:T(8,128)}, u32[]{:S(2)}, u32[]{:S(2)}) collective-permute-start(f32[40,2048]{1,0:T(8,128)} %copy-done.17), channel_id=1, source_target_pairs={{0,1},{1,2},{2,3},{3,4},{4,5},{5,6},{6,7},{7,8},{8,9},{9,10},{10,1... | collective-permute-start | bytes 983048 | tf_op jit(solution)/shard_map/ppermute | solution.py:350
  51.5 4.5 %collective-permute-start.1 = (f32[40,2048]{1,0:T(8,128)}, f32[40,2048]{1,0:T(8,128)}, u32[]{:S(2)}, u32[]{:S(2)}) collective-permute-start(f32[40,2048]{1,0:T(8,128)} %copy-done.17), channel_id=1, source_target_pairs={{1,0},{2,1},{3,2},{4,3},{5,4},{6,5},{7,6},{8,7},{9,8},{10,9},{11,1... | collective-permute-start | bytes 983048 | tf_op jit(solution)/shard_map/ppermute | solution.py:350
  56.0 1.4 reshape.76
  58.1 1.4 copy.24
  59.5 1.4 reshape.82
  61.5 0.8 copy.23
  67.2 1.9 %convert_reduce_fusion.1 = (s32[4]{0:T(128)}, pred[4,128]{1,0:T(4,128)(4,1)S(1)}, s32[4,128]{1,0:T(4,128)}) fusion(s32[]{:T(128)} %axis_index.25, s32[512,128]{1,0:T(8,128)} %param.30, s32[]{:T(128)S(6)} %select_n.24, s32[4]{0:T(128)S(1)} %dynamic_slice.10), kind=kLoop, calls=%fused_computation.15 | loop fusion | flops 12284 | bytes 4648 | tf_op jit(solution)/shard_map/reduce_sum | solution.py:437
  71.0 0.9 pad_maximum_fusion.cl_own_ref
  71.9 8.0 %collective-permute-start.2 = (f32[152,128]{1,0:T(8,128)S(1)}, f32[152,128]{1,0:T(8,128)S(1)}, u32[]{:S(2)}, u32[]{:S(2)}) collective-permute-start(f32[152,128]{1,0:T(8,128)S(1)} %pad_maximum_fusion.cl_own_ref), channel_id=1, source_target_pairs={{0,4},{4,8},{8,12},{12,16},{16,20},{20,24},{24,28},{28,32},{32,36}... | collective-permute-start | bytes 233480 | tf_op jit(solution)/shard_map/ppermute | solution.py:356
  79.9 1.9 %collective-permute-start.3 = (f32[152,128]{1,0:T(8,128)S(1)}, f32[152,128]{1,0:T(8,128)S(1)}, u32[]{:S(2)}, u32[]{:S(2)}) collective-permute-start(f32[152,128]{1,0:T(8,128)S(1)} %pad_maximum_fusion.cl_own_ref), channel_id=1, source_target_pairs={{4,0},{8,4},{12,8},{16,12},{20,16},{24,20},{28,24},{32,28},{36,32}... | collective-permute-start | bytes 233480 | tf_op jit(solution)/shard_map/ppermute | solution.py:356
  81.9 0.9 select_reduce_fusion
  82.8 6.8 %collective-permute-done.3.cl_after_ref = f32[152,128]{1,0:T(8,128)S(1)} collective-permute-done((f32[152,128]{1,0:T(8,128)S(1)}, f32[152,128]{1,0:T(8,128)S(1)}, u32[]{:S(2)}, u32[]{:S(2)}) %collective-permute-start.3) | collective-permute-done | bytes 77856 | tf_op jit(solution)/shard_map/ppermute | solution.py:356
  89.6 1.0 copy-done.18
  90.6 26.0 %shard_map.155 = (f32[16,2048]{1,0:T(8,128)S(1)}, f32[16,2048]{1,0:T(8,128)S(1)}, f32[32,128]{1,0:T(8,128)S(1)}, s32[16,128]{1,0:T(8,128)S(1)}) custom-call(s32[864]{0:T(1024)S(1)} %copy-done.10, s32[768]{0:T(1024)S(1)} %copy-done.9, s32[256]{0:T(256)S(1)} %copy-done.16, s32[1]{0:T(128)} %bitcast.4.sub_pos, s32[1,2048]{1,0:T(1,128)S(1)} %copy-done.5, ...), custom_call_target="tpu_custom_call" | custom-call | flops 140000000 | bytes 4194304 | tf_op jit(solution)/shard_map/pallas_call | solution.py:336
  119.1 6.4 %shard_map.156 = f32[64,128]{1,0:T(8,128)S(1)} custom-call(s32[512]{0:T(512)S(1)} %bitcast.7, s32[4]{0:T(128)S(1)} %copy-done.15, f32[128,1,1280]{2,1,0:T(1,128)S(1)} %all-to-all-done.1.source_ref, f32[4,8,128]{2,1,0:T(8,128)S(1)} %pad.4.target_ref, f32[32,128]{1,0:T(8,128)S(1)} %copy-done.3), custom_call_target="tpu_custom_call" | custom-call | bytes 4194304 | tf_op jit(solution)/shard_map/pallas_call | solution.py:336
  125.6 7.0 %all_to_all.21.group_ref = f32[4,64,128]{2,1,0:T(8,128)S(1)} all-to-all(f32[4,64,128]{2,1,0:T(8,128)S(1)} %broadcast_in_dim.44), channel_id=1, replica_groups=mesh['leaf'=128,'sub'=4] {'sub'}, dimensions={0} | all-to-all | bytes 262144 | tf_op jit(solution)/shard_map/all_to_all | solution.py:446
  133.2 8.6 %shard_map.157 = f32[16,2048]{1,0:T(8,128)} custom-call(s32[32]{0:T(128)S(1)} %copy-done.14, s32[16]{0:T(128)S(1)} %copy-done.12, f32[4,64,128]{2,1,0:T(8,128)S(1)} %all_to_all.21.group_ref, f32[16,2048]{1,0:T(8,128)S(1)} %get-tuple-element.16.near_ref, f32[16,2048]{1,0:T(8,128)S(1)} %get-tuple-element.17.far_ref, s32[16,128]{1,0:T(8,128)S(1)} %copy-done.7, ...), custom_call_target="tpu_custom_call" | custom-call | bytes 4194304 | tf_op jit(solution)/shard_map/pallas_call | solution.py:336
  (89 shorter events, 17.2 us)
Async XLA Ops:
  0.0 1.5 %copy-start.19 = (f32[32,4096]{1,0:T(8,128)S(1)}, f32[32,4096]{1,0:T(8,128)}, u32[]{:S(2)}) copy-start(f32[32,4096]{1,0:T(8,128)} %param.23) | copy-start | bytes 1572868
  1.5 1.0 copy-start.20
  2.5 0.8 copy-start.21
  3.2 1.9 %copy-start = (f32[16,2048]{1,0:T(8,128)S(1)}, f32[16,2048]{1,0:T(8,128)}, u32[]{:S(2)}) copy-start(f32[16,2048]{1,0:T(8,128)} %x_ref.1) | copy-start | bytes 393220
  3.4 1.8 %copy-start.1 = (f32[3,2048]{1,0:T(4,128)S(1)}, f32[3,2048]{1,0:T(4,128)}, u32[]{:S(2)}) copy-start(f32[3,2048]{1,0:T(4,128)} %points_ref.1) | copy-start | bytes 73732
  3.4 1.8 %copy-start.4 = (s32[1,2048]{1,0:T(1,128)S(1)}, s32[1,2048]{1,0:T(1,128)}, u32[]{:S(2)}) copy-start(s32[1,2048]{1,0:T(1,128)} %order_ref.3) | copy-start | bytes 24580
  5.1 5.3 %copy-start.13 = (s32[32]{0:T(128)}, s32[32]{0:T(128)S(1)}, u32[]{:S(2)}) copy-start(s32[32]{0:T(128)S(1)} %broadcast_subtract_fusion.2.leaf_slot) | copy-start | bytes 388
  18.1 9.4 %all-to-all-start.2 = ((f32[4,128,128]{2,1,0:T(8,128)}), f32[4,128,128]{2,1,0:T(8,128)S(1)}, u32[]{:S(2)}, u32[]{:S(2)}) async-start(f32[4,128,128]{2,1,0:T(8,128)} %broadcast_in_dim.43), calls=%async_computation.2 | async-start | bytes 524288 | tf_op jit(solution)/shard_map/all_to_all | solution.py:392
  28.7 89.0 %all-to-all-start.1 = ((f32[128,1,1280]{2,1,0:T(1,128)}), f32[128,1,1280]{2,1,0:T(1,128)S(1)}, u32[]{:S(2)}, u32[]{:S(2)}) async-start(f32[128,1,1280]{2,1,0:T(1,128)} %broadcast_in_dim.42), calls=%async_computation.1 | async-start | bytes 1310720 | tf_op jit(solution)/shard_map/all_to_all | solution.py:386
  49.6 7.9 %copy-start.22 = (f32[16,192]{1,0:T(8,128)S(1)}, f32[16,192]{1,0:T(8,128)}, u32[]{:S(2)}) copy-start(f32[16,192]{1,0:T(8,128)} %param.25) | copy-start | bytes 36868
  49.6 40.0 %collective-permute-start = (f32[40,2048]{1,0:T(8,128)}, f32[40,2048]{1,0:T(8,128)}, u32[]{:S(2)}, u32[]{:S(2)}) collective-permute-start(f32[40,2048]{1,0:T(8,128)} %copy-done.17), channel_id=1, source_target_pairs={{0,1},{1,2},{2,3},{3,4},{4,5},{5,6},{6,7},{7,8},{8,9},{9,10},{10,1... | collective-permute-start | bytes 983048 | tf_op jit(solution)/shard_map/ppermute | solution.py:350
  51.5 38.0 %collective-permute-start.1 = (f32[40,2048]{1,0:T(8,128)}, f32[40,2048]{1,0:T(8,128)}, u32[]{:S(2)}, u32[]{:S(2)}) collective-permute-start(f32[40,2048]{1,0:T(8,128)} %copy-done.17), channel_id=1, source_target_pairs={{1,0},{2,1},{3,2},{4,3},{5,4},{6,5},{7,6},{8,7},{9,8},{10,9},{11,1... | collective-permute-start | bytes 983048 | tf_op jit(solution)/shard_map/ppermute | solution.py:350
  59.5 1.4 %copy-start.23 = (s32[32,24]{0,1:T(8,128)S(1)}, s32[32,24]{0,1:T(8,128)}, u32[]{:S(2)}) copy-start(s32[32,24]{0,1:T(8,128)} %param.21) | copy-start | bytes 9220
  71.0 10.9 %copy-start.24 = (s32[4,128]{1,0:T(4,128)S(1)}, s32[4,128]{1,0:T(4,128)}, u32[]{:S(2)}) copy-start(s32[4,128]{1,0:T(4,128)} %convert_reduce_fusion) | copy-start | bytes 6148
  71.0 10.9 %copy-start.25 = (s32[4,128]{1,0:T(4,128)S(1)}, s32[4,128]{1,0:T(4,128)}, u32[]{:S(2)}) copy-start(s32[4,128]{1,0:T(4,128)} %get-tuple-element.21) | copy-start | bytes 6148
  71.0 10.9 %copy-start.27 = (pred[4,128]{1,0:T(4,128)(4,1)S(1)}, pred[4,128]{1,0:T(4,128)(4,1)}, u32[]{:S(2)}) copy-start(pred[4,128]{1,0:T(4,128)(4,1)} %copy-done.26) | copy-start | bytes 1540
  71.0 18.5 %copy-start.9 = (s32[768]{0:T(1024)S(1)}, s32[768]{0:T(1024)}, u32[]{:S(2)}) copy-start(s32[768]{0:T(1024)} %reshape.78.far_ids) | copy-start | bytes 9220
  71.0 18.5 %copy-start.10 = (s32[864]{0:T(1024)S(1)}, s32[864]{0:T(1024)}, u32[]{:S(2)}) copy-start(s32[864]{0:T(1024)} %reshape.77.near_ids) | copy-start | bytes 10372
  71.9 17.7 %copy-start.5 = (s32[1,2048]{1,0:T(1,128)S(1)}, s32[1,2048]{1,0:T(1,128)}, u32[]{:S(2)}) copy-start(s32[1,2048]{1,0:T(1,128)} %order_ref.3) | copy-start | bytes 24580
  71.9 10.9 %collective-permute-start.2 = (f32[152,128]{1,0:T(8,128)S(1)}, f32[152,128]{1,0:T(8,128)S(1)}, u32[]{:S(2)}, u32[]{:S(2)}) collective-permute-start(f32[152,128]{1,0:T(8,128)S(1)} %pad_maximum_fusion.cl_own_ref), channel_id=1, source_target_pairs={{0,4},{4,8},{8,12},{12,16},{16,20},{20,24},{24,28},{28,32},{32,36}... | collective-permute-start | bytes 233480 | tf_op jit(solution)/shard_map/ppermute | solution.py:356
  79.9 9.6 %collective-permute-start.3 = (f32[152,128]{1,0:T(8,128)S(1)}, f32[152,128]{1,0:T(8,128)S(1)}, u32[]{:S(2)}, u32[]{:S(2)}) collective-permute-start(f32[152,128]{1,0:T(8,128)S(1)} %pad_maximum_fusion.cl_own_ref), channel_id=1, source_target_pairs={{4,0},{8,4},{12,8},{16,12},{20,16},{24,20},{28,24},{32,28},{36,32}... | collective-permute-start | bytes 233480 | tf_op jit(solution)/shard_map/ppermute | solution.py:356
  82.8 6.8 %copy-start.16 = (s32[256]{0:T(256)S(1)}, s32[256]{0:T(256)}, u32[]{:S(2)}) copy-start(s32[256]{0:T(256)} %reshape.79.cluster_ids) | copy-start | bytes 3076
  89.6 1.0 copy-start.18
  125.6 7.0 %copy-start.7 = (s32[16,128]{1,0:T(8,128)S(1)}, s32[16,128]{1,0:T(8,128)}, u32[]{:S(2)}) copy-start(s32[16,128]{1,0:T(8,128)} %copy-done.6) | copy-start | bytes 24580
  (12 other events, 7.5 us)
where the time goes:
time: 143 us; the launch traced here: 142 us
  Pallas kernels  46.3 us (32%)
  starting transfers between devices  40.7 us (28%)
  local copies, waits for them, and re-layouts  22.3 us (16%)
  blocking collectives  13.2 us (9%)
  waiting for transfers between devices  12 us (8%)
  other arithmetic  7.12 us (5%)
    pallas_call x4, Pallas kernels, call(): pl.pallas_call(body, in_specs=[SMEM] * len(scalars) + [VMEM] * len(arrays...  46.3 us
    all_to_all x1, starting transfers between devices, local(): lax.all_to_all(jnp.broadcast_to(top_load[None], (leaf_count, 1, 10 * TILE...  20.8 us
    ppermute x2, starting transfers between devices, leaf_shift(): return lax.ppermute(value, 'leaf', pairs)  9.96 us
    unnamed x60, local copies, waits for them, and re-layouts  8.21 us
    all_to_all x1, blocking collectives, local(): lax.all_to_all(jnp.broadcast_to(share, (SUB, (C2 + C1 // SUB) * 8, TILE))...  7.02 us
    ppermute x2, waiting for transfers between devices, leaf_shift(): return lax.ppermute(value, 'leaf', pairs)  6.78 us
    ppermute x2, starting transfers between devices, linear_shift(): return lax.ppermute(value, ('leaf', 'sub'), pairs)  6.46 us
    all_to_all x1, blocking collectives, local(): s2 = lax.all_to_all(s2_part.reshape(SUB, 8, TILE), 'sub', 0, 0).sum(axis=0)  6.2 us
  transfers between devices with their start and end apart: 6, of which 2 were waited for; matrix products, arithmetic and copies ran while one was open for 12% of the time, Pallas kernels for 18%

commit v1 on v0

v1 whole, which is shorter than its diff:
```python
import functools

import jax
import jax.numpy as jnp
from jax import lax
from jax.experimental import pallas as pl
from jax.experimental.pallas import tpu as pltpu
from jax.sharding import PartitionSpec as P

COLS = 16
LEAF = 64
RANK = 64
NB = 27
RN = 16
RF = 32
F0 = 24
F1 = 16
C2 = 4
MAXF2 = 128
LD = 32
C1 = 16
SUB = 4
PTS = LD * LEAF
TILE = 128
ROWS = 40
GROUP = 4

INV_FOUR_PI = 0.07957747154594767
SOFTENING = 0.0025
F32 = jnp.float32
BF16 = jnp.bfloat16
VMEM_LIMIT = 48 * 1024 * 1024


def split(value):
    high = value.astype(BF16)
    low = (value - high.astype(F32)).astype(BF16)
    return high, low


def small_dot(lhs, rhs, transposed=False):
    dims = (((1,), (1,)), ((), ())) if transposed else (((1,), (0,)), ((), ()))
    rows = lhs.shape[0]
    lhs_high, lhs_low = split(lhs)
    rhs_high, rhs_low = split(rhs)
    both = jnp.concatenate([lhs_high, lhs_low], axis=0)
    first = lax.dot_general(both, rhs_high, dims, preferred_element_type=F32)
    second = lax.dot_general(lhs_high, rhs_low, dims, preferred_element_type=F32)
    return first[:rows] + first[rows:] + second


def permuted(read, index_rows, write):
    for out_tile in range(PTS // TILE):
        index = jnp.broadcast_to(index_rows(out_tile), (8, TILE))
        lane = index & (TILE - 1)
        source = index >> 7
        for half in range(2):
            total = jnp.zeros((8, TILE), F32)
            for tile in range(PTS // TILE):
                picked = jnp.take_along_axis(read(half, tile), lane, axis=1, mode="promise_in_bounds")
                total = jnp.where(source == tile, picked, total)
            write(half, out_tile, total)


def to_tile(value):
    return jnp.concatenate([value[:8], value[8:]], axis=1)


def from_tile(tile):
    return jnp.concatenate([tile[:, :RANK], tile[:, RANK:]], axis=0)


def fetched(sources, targets, sems):
    copies = [
        pltpu.make_async_copy(source, target, sems.at[k])
        for k, (source, target) in enumerate(zip(sources, targets))
    ]
    for copy in copies:
        copy.start()
    return copies


def quarter(value, k):
    lane = lax.broadcasted_iota(jnp.int32, value.shape, 1)
    return jnp.where(lane // RANK == k, value, 0.0)


def group_up(natural, mats):
    blocks = jnp.concatenate([quarter(natural, k) for k in range(GROUP)], axis=0)
    return small_dot(blocks, mats)


def group_down(parts, mats):
    wide = small_dot(jnp.concatenate(parts, axis=0), mats, True)
    lane = lax.broadcasted_iota(jnp.int32, (COLS, GROUP * RANK), 1) // RANK
    total = wide[:COLS]
    for k in range(1, GROUP):
        total = jnp.where(lane == k, wide[k * COLS : (k + 1) * COLS], total)
    return total


def joined(parts):
    return jnp.concatenate(parts, axis=1)


def skeleton_rows(ref, pair):
    first, second = ref[2 * pair : 2 * pair + 1, :], ref[2 * pair + 1 : 2 * pair + 2, :]
    return [
        joined([first[:, k * RANK : (k + 1) * RANK], second[:, k * RANK : (k + 1) * RANK]])
        for k in range(3)
    ]


def upward_kernel(
    base, x_any, order_any, points_any, skel_any, leaf_any, cluster_any, basis_ref, transfer_ref,
    cluster_transfer_ref, pay_ref, send_ref, s1_acc, s2_acc,
    x_ref, order_ref, points_ref, skel_ref, leaf_parent, cluster_parent, sems,
):
    copies = fetched(
        [x_any, order_any, points_any, skel_any, leaf_any, cluster_any],
        [x_ref, order_ref, points_ref, skel_ref, leaf_parent, cluster_parent],
        sems,
    )
    for copy in copies:
        copy.wait()

    def read(half, tile):
        return x_ref[half * 8 : half * 8 + 8, tile * TILE : (tile + 1) * TILE]

    def write(half, tile, value):
        pay_ref[half * 8 : half * 8 + 8, tile * TILE : (tile + 1) * TILE] = value

    permuted(read, lambda tile: order_ref[:, tile * TILE : (tile + 1) * TILE], write)
    pay_ref[32:35, :] = points_ref[...]
    pay_ref[38:40, :] = jnp.zeros((2, PTS), F32)
    for pair in range(LD // 2):
        for k, row in enumerate(skeleton_rows(skel_ref, pair)):
            pay_ref[35 + k : 36 + k, pair * TILE : (pair + 1) * TILE] = row
    s1_acc[...] = jnp.zeros_like(s1_acc)
    s2_acc[...] = jnp.zeros_like(s2_acc)
    width = GROUP * LEAF
    coefs = []
    for group in range(LD // GROUP):
        values = pay_ref[:16, group * width : (group + 1) * width]
        mats = basis_ref[group * GROUP : (group + 1) * GROUP].reshape(width, RANK)
        out = group_up(values, mats)
        natural = joined([out[k * COLS : (k + 1) * COLS] for k in range(GROUP)])
        pay_ref[16:32, group * width : (group + 1) * width] = natural
        coefs.append(natural)
    ups = []
    for group in range(LD // GROUP):
        mats = transfer_ref[group * GROUP : (group + 1) * GROUP].reshape(width, RANK)
        ups.append(group_up(coefs[group], mats))
    for leaf in range(LD):
        slot = leaf_parent[leaf] - base[0]
        at = leaf % GROUP * COLS
        s1_acc[slot] = s1_acc[slot] + ups[leaf // GROUP][at : at + COLS]
    ups = []
    for group in range(C1 // GROUP):
        parts = [s1_acc[group * GROUP + k] for k in range(GROUP)]
        mats = cluster_transfer_ref[group * GROUP : (group + 1) * GROUP].reshape(width, RANK)
        ups.append(group_up(joined(parts), mats))
        for k in range(GROUP):
            at = 8 + (group * GROUP + k) * 8
            tile = to_tile(parts[k])
            for peer in range(SUB):
                send_ref[peer, at : at + 8, :] = tile
    for cluster in range(C1):
        slot = cluster_parent[cluster] - base[1]
        at = cluster % GROUP * COLS
        s2_acc[slot] = s2_acc[slot] + ups[cluster // GROUP][at : at + COLS]
    for top in range(C2):
        send_ref[top, 0:8, :] = to_tile(s2_acc[top])


def middle_kernel(
    base, before_any, after_any, received_ref, cluster_skel_ref, top_skel_ref, cluster_ref, top_ref
):
    del before_any, after_any
    total = received_ref[0]
    for peer in range(1, SUB):
        total = total + received_ref[peer]
    cluster_ref[0:TILE, :] = total[8:]
    for pair in range(C1 // 2):
        for k, row in enumerate(skeleton_rows(cluster_skel_ref, pair)):
            cluster_ref[TILE + 8 * k + pair : TILE + 8 * k + pair + 1, :] = row
    which = lax.broadcasted_iota(jnp.int32, (C2, 3 * RANK), 0)
    skel = jnp.sum(jnp.where(which == base[3], top_skel_ref[...], 0.0), axis=0, keepdims=True)
    load = joined([total[j : j + 1] for j in range(8)] + [skel, jnp.zeros((1, RANK), F32)])
    top_ref[...] = jnp.broadcast_to(load[None], top_ref.shape)


def source_pair(first, second):
    lane = lax.broadcasted_iota(jnp.int32, (8, TILE), 1)
    return jnp.where(lane < RANK, first, second)


def green(target, source):
    dx = target[0] - source[0:1]
    dy = target[1] - source[1:2]
    dz = target[2] - source[2:3]
    return lax.rsqrt(dx * dx + dy * dy + dz * dz + SOFTENING)


def spread(columns):
    return [jnp.broadcast_to(columns[:, k : k + 1], (LEAF, TILE)) for k in range(3)]


def quad_product(target, sources, weights):
    high, low = [], []
    for first, second in ((0, 1), (2, 3)):
        block = green(target, source_pair(sources[first], sources[second]))
        block_high, block_low = split(block)
        high.append(block_high)
        low.append(block_low)
    lhs = jnp.concatenate(
        [jnp.concatenate(high, axis=1), jnp.concatenate(low, axis=1)], axis=0
    )
    rhs = jnp.concatenate(weights, axis=0)
    return jnp.dot(lhs, rhs, preferred_element_type=F32)


def listed_product(target, indices, place_ref, weight_ref):
    total = None
    for quad in range(len(indices) // 4):
        group = indices[quad * 4 : quad * 4 + 4]
        part = quad_product(target, [place_ref[i] for i in group], [weight_ref[i] for i in group])
        total = part if total is None else total + part
    return total[:LEAF] + total[LEAF:]


def weights_of(values):
    high = values.astype(BF16).astype(F32)
    low = values - high
    return jnp.concatenate([high, low], axis=0).T.astype(BF16)


def stage_pair(pay, row_value, row_place, tile, place_ref, weight_ref, slot):
    lanes = slice(tile * TILE, (tile + 1) * TILE)
    weights = weights_of(pay[row_value : row_value + 16, lanes])
    weight_ref[slot] = weights[:LEAF]
    weight_ref[slot + 1] = weights[LEAF:]
    place = pay[row_place : row_place + 3, lanes]
    swapped = pltpu.roll(place, RANK, 1)
    lane = lax.broadcasted_iota(jnp.int32, (3, TILE), 1)
    place_ref[slot, 0:3] = jnp.where(lane < RANK, place, swapped)
    place_ref[slot + 1, 0:3] = jnp.where(lane < RANK, swapped, place)


def finish_rows(result_ref, count, write):
    for pair in range(count // 2):
        block = result_ref[pair * TILE : (pair + 1) * TILE, :].T
        write(pair, (block[:16] + block[16:]) * INV_FOUR_PI)


def interaction_kernel(
    base, order_any, near_any, far_any, own_ref, before_ref, after_ref,
    near_ref, far_ref, inverse_ref,
    near_place, near_weight, far_place, far_weight, target_cols, near_rows, far_rows,
    order_ref, near_ids, far_ids, sems,
):
    copies = fetched([order_any, near_any, far_any], [order_ref, near_ids, far_ids], sems)
    tiles = PTS // TILE
    for tile in range(tiles):
        stage_pair(own_ref, 0, 32, tile, near_place, near_weight, RN + 2 * tile)
        stage_pair(own_ref, 16, 35, tile, far_place, far_weight, LD + 2 * tile)
    for tile in range(tiles):
        block = own_ref[32:40, tile * TILE : (tile + 1) * TILE].T
        target_cols[2 * tile] = block[:LEAF]
        target_cols[2 * tile + 1] = block[LEAF:]
    for copy in copies:
        copy.wait()
    for tile in range(tiles // 2):
        stage_pair(before_ref, 0, 32, tiles // 2 + tile, near_place, near_weight, 2 * tile)
        stage_pair(after_ref, 0, 32, tile, near_place, near_weight, RN + LD + 2 * tile)
    for tile in range(tiles):
        stage_pair(before_ref, 16, 35, tile, far_place, far_weight, 2 * tile)
        stage_pair(after_ref, 16, 35, tile, far_place, far_weight, 2 * LD + 2 * tile)
    near_weight[2 * RN + LD] = jnp.zeros((LEAF, 32), BF16)
    near_place[2 * RN + LD, 0:3] = jnp.zeros((3, TILE), F32)

    def leaf_step(leaf, carry):
        columns = target_cols[leaf]
        target = spread(columns)
        ids = [near_ids[leaf, k] - base[2] + RN for k in range(NB)] + [2 * RN + LD]
        near_rows[pl.ds(leaf * LEAF, LEAF), :] = listed_product(target, ids, near_place, near_weight)
        target = spread(columns[:, 3:6])
        ids = [far_ids[leaf, k] - base[2] + RF for k in range(F0)]
        far_rows[pl.ds(leaf * LEAF, LEAF), :] = listed_product(target, ids, far_place, far_weight)
        return carry

    lax.fori_loop(0, LD, leaf_step, 0, unroll=2)

    def write_near(pair, block):
        near_ref[:, pair * TILE : (pair + 1) * TILE] = block

    def write_far(pair, block):
        far_ref[:, pair * TILE : (pair + 1) * TILE] = block

    finish_rows(near_rows, LD, write_near)
    finish_rows(far_rows, LD, write_far)

    order = order_ref[...]
    position = lax.broadcasted_iota(jnp.int32, (16, PTS), 1)
    hit = (order >> 7) == lax.broadcasted_iota(jnp.int32, (16, PTS), 0)
    coarse = jnp.where(hit, (position >> 7).astype(F32), 0.0)
    fine = jnp.where(hit, (position & (TILE - 1)).astype(F32), 0.0)
    lhs = jnp.concatenate([coarse, fine], axis=0).astype(BF16)
    lane_of = (order & (TILE - 1)) == lax.broadcasted_iota(jnp.int32, (TILE, PTS), 0)
    rhs = jnp.where(lane_of, 1.0, 0.0).astype(BF16)
    found = lax.dot_general(lhs, rhs, (((1,), (1,)), ((), ())), preferred_element_type=F32)
    inverse_ref[...] = found[:16].astype(jnp.int32) * TILE + found[16:].astype(jnp.int32)


def write_tiles(rows_ref, count, out_ref, start):
    def write(pair, block):
        at = start + pair * 16
        out_ref[at : at + 8, :] = to_tile(block[:, :RANK])
        out_ref[at + 8 : at + 16, :] = to_tile(block[:, RANK:])

    finish_rows(rows_ref, count, write)


def cluster_kernel(
    base, near_any, cluster_any, own_ref, before_ref, after_ref,
    z1_ref, cl_place, cl_weight, cl_rows, cluster_ids, sems,
):
    del near_any
    copies = fetched([cluster_any], [cluster_ids], sems)
    for part, ref in enumerate((before_ref, own_ref, after_ref)):
        for cluster in range(C1):
            tile = ref[cluster * 8 : cluster * 8 + 8, :]
            cl_weight[part * C1 + cluster] = weights_of(from_tile(tile))
        for pair in range(C1 // 2):
            slot = part * C1 + 2 * pair
            place = jnp.concatenate(
                [ref[TILE + 8 * k + pair : TILE + 8 * k + pair + 1, :] for k in range(3)], axis=0
            )
            swapped = pltpu.roll(place, RANK, 1)
            lane = lax.broadcasted_iota(jnp.int32, (3, TILE), 1)
            cl_place[slot, 0:3] = jnp.where(lane < RANK, place, swapped)
            cl_place[slot + 1, 0:3] = jnp.where(lane < RANK, swapped, place)

    for copy in copies:
        copy.wait()

    def cluster_step(k, carry):
        mine = base[3] * (C1 // SUB) + k
        columns = cl_place[C1 + mine].T
        target = spread(columns[:LEAF])
        ids = [cluster_ids[mine, j] - base[0] + C1 for j in range(F1)]
        cl_rows[pl.ds(k * LEAF, LEAF), :] = listed_product(target, ids, cl_place, cl_weight)
        return carry

    lax.fori_loop(0, C1 // SUB, cluster_step, 0, unroll=2)
    write_tiles(cl_rows, C1 // SUB, z1_ref, 0)


def top_kernel(
    base, counts_any, table_any, target_any, source_ref, z1_ref,
    out_ref, rows, lists, top_counts, table, target_ref, sems,
):
    aligned = pl.multiple_of(base[1] // 8 * 8, 8)
    copies = fetched(
        [counts_any, table_any.at[pl.ds(aligned, 8)], target_any], [top_counts, table, target_ref], sems
    )
    out_ref[C2 * 8 :, :] = z1_ref[...]
    for copy in copies:
        copy.wait()
    def scan(top):
        def note(slot, found):
            cluster = table[base[1] - aligned + top, slot]
            lists[top, found] = cluster // SUB
            return found + jnp.where(cluster % SUB == base[3], 1, 0)

        return lax.fori_loop(0, top_counts[base[1] + top], note, 0)

    for top in range(C2):
        found = scan(top)
        skel = jnp.concatenate(
            [target_ref[top : top + 1, k * RANK : (k + 1) * RANK] for k in range(3)]
            + [jnp.zeros((5, RANK), F32)],
            axis=0,
        )
        columns = joined([skel, jnp.zeros((8, RANK), F32)]).T
        target = spread(columns[:LEAF])
        where = slice(top * LEAF, (top + 1) * LEAF)
        rows[where, :] = jnp.zeros((LEAF, 32), F32)

        def step(quad, carry, target=target, found=found, where=where, top=top):
            places, weights = [], []
            lane = lax.broadcasted_iota(jnp.int32, (1, TILE), 1)
            for k in range(GROUP):
                at = GROUP * quad + k
                live = at < found
                source = jnp.where(live, lists[top, jnp.where(live, at, 0)], 0)
                tile = jnp.concatenate(
                    [source_ref[source, :, j * TILE : (j + 1) * TILE] for j in range(8)], axis=0
                )
                weights.append(weights_of(from_tile(tile) * jnp.where(live, 1.0, 0.0).astype(F32)))
                first = source_ref[source, :, 8 * TILE : 9 * TILE]
                second = source_ref[source, :, 9 * TILE : 10 * TILE]
                places.append((first, second))
            high, low = [], []
            for (a0, a1), (b0, b1) in ((places[0], places[1]), (places[2], places[3])):
                rows_of = [
                    jnp.where(lane < RANK, a0, pltpu.roll(b0, RANK, 1)),
                    jnp.where(lane < RANK, pltpu.roll(a0, RANK, 1), b0),
                    jnp.where(lane < RANK, a1, pltpu.roll(b1, RANK, 1)),
                ]
                block_high, block_low = split(green(target, jnp.concatenate(rows_of, axis=0)))
                high.append(block_high)
                low.append(block_low)
            lhs = jnp.concatenate([joined(high), joined(low)], axis=0)
            part = jnp.dot(lhs, jnp.concatenate(weights, axis=0), preferred_element_type=F32)
            rows[where, :] = rows[where, :] + part[:LEAF] + part[LEAF:]
            return carry

        lax.fori_loop(0, (found + GROUP - 1) // GROUP, step, 0)
    write_tiles(rows, C2, out_ref, 0)


def downward_kernel(
    base, leaf_any, cluster_any, group_ref, near_ref, far_ref, inverse_ref, basis_ref,
    transfer_ref, cluster_transfer_ref, out_ref, z2_acc, w1_acc, morton,
    leaf_parent, cluster_parent, sems,
):
    copies = fetched([leaf_any, cluster_any], [leaf_parent, cluster_parent], sems)
    for top in range(C2):
        tile = group_ref[0, top * 8 : top * 8 + 8, :]
        for part in range(1, SUB):
            tile = tile + group_ref[part, top * 8 : top * 8 + 8, :]
        z2_acc[top] = from_tile(tile)
    for copy in copies:
        copy.wait()
    width = GROUP * RANK
    for group in range(C1 // GROUP):
        parts = [z2_acc[cluster_parent[group * GROUP + k] - base[1]] for k in range(GROUP)]
        mats = cluster_transfer_ref[group * GROUP : (group + 1) * GROUP].reshape(width, RANK)
        wide = small_dot(jnp.concatenate(parts, axis=0), mats, True)
        for k in range(GROUP):
            cluster = group * GROUP + k
            part, place = divmod(cluster, C1 // SUB)
            at = C2 * 8 + place * 8
            local = from_tile(group_ref[part, at : at + 8, :])
            w1_acc[cluster] = local + wide[k * COLS : (k + 1) * COLS, k * RANK : (k + 1) * RANK]
    locals_ = []
    for group in range(LD // GROUP):
        parts = [w1_acc[leaf_parent[group * GROUP + k] - base[0]] for k in range(GROUP)]
        mats = transfer_ref[group * GROUP : (group + 1) * GROUP].reshape(width, RANK)
        down = group_down(parts, mats)
        locals_.append(far_ref[:, group * width : (group + 1) * width] + down)
    for group in range(LD // GROUP):
        parts = [locals_[group][:, k * RANK : (k + 1) * RANK] for k in range(GROUP)]
        mats = basis_ref[group * GROUP : (group + 1) * GROUP].reshape(width, RANK)
        lanes = slice(group * width, (group + 1) * width)
        morton[:, lanes] = near_ref[:, lanes] + group_down(parts, mats)

    def read(half, tile):
        return morton[half * 8 : half * 8 + 8, tile * TILE : (tile + 1) * TILE]

    def write(half, tile, value):
        out_ref[half * 8 : half * 8 + 8, tile * TILE : (tile + 1) * TILE] = value

    permuted(read, lambda tile: inverse_ref[tile : tile + 1, :], write)


SMEM = pl.BlockSpec(memory_space=pltpu.SMEM)
VMEM = pl.BlockSpec(memory_space=pltpu.VMEM)
ANY = pl.BlockSpec(memory_space=pl.ANY)


def call(body, scalars, anywhere, arrays, outs, scratch, flops=0, trans=0, loose=()):
    placed = list(loose)
    placed += [pltpu.with_memory_space_constraint(array, pltpu.HBM) for array in anywhere]
    placed += [pltpu.with_memory_space_constraint(array, pltpu.VMEM) for array in arrays]
    return pl.pallas_call(
        body,
        in_specs=[SMEM] * len(scalars) + [ANY] * (len(loose) + len(anywhere)) + [VMEM] * len(arrays),
        out_specs=[VMEM] * len(outs),
        out_shape=[jax.ShapeDtypeStruct(shape, dtype) for shape, dtype in outs],
        scratch_shapes=scratch,
        compiler_params=pltpu.CompilerParams(vmem_limit_bytes=VMEM_LIMIT),
        cost_estimate=pl.CostEstimate(flops=flops, bytes_accessed=4 * 1024 * 1024, transcendentals=trans),
    )(*scalars, *placed)


def linear_shift(value, step):
    size = lax.axis_size("leaf") * lax.axis_size("sub")
    pairs = [(i, i + step) for i in range(size) if 0 <= i + step < size]
    return lax.ppermute(value, ("leaf", "sub"), pairs)


def leaf_shift(value, step):
    size = lax.axis_size("leaf")
    pairs = [(i, i + step) for i in range(size) if 0 <= i + step < size]
    return lax.ppermute(value, "leaf", pairs)


def local(
    x_user, morton_order, points, leaf_basis, near_list, far_leaf, leaf_skeleton, leaf_transfer,
    leaf_parent, cluster_skeleton, far_cluster, cluster_transfer, cluster_parent, top_skeleton,
    far_top, top_counts,
):
    leaf_count = lax.axis_size("leaf")
    leaf_pos = lax.axis_index("leaf")
    sub_pos = lax.axis_index("sub")
    first_leaf = (leaf_pos * SUB + sub_pos) * LD
    base = jnp.stack([leaf_pos * C1, leaf_pos * C2, first_leaf, sub_pos]).astype(jnp.int32)
    basis = leaf_basis.reshape(LD, LEAF, RANK)
    transfer = leaf_transfer.reshape(LD, RANK, RANK)
    cluster_trans = cluster_transfer.reshape(C1, RANK, RANK)

    pay, send = call(
        upward_kernel,
        [base],
        [x_user, morton_order, points, leaf_skeleton, leaf_parent, cluster_parent],
        [basis, transfer, cluster_trans],
        [((ROWS, PTS), F32), ((SUB, 8 + C1 * 8, TILE), F32)],
        [
            pltpu.VMEM((C1, COLS, RANK), F32),
            pltpu.VMEM((C2, COLS, RANK), F32),
            pltpu.VMEM((COLS, PTS), F32),
            pltpu.VMEM((1, PTS), jnp.int32),
            pltpu.VMEM((3, PTS), F32),
            pltpu.VMEM((LD, 3 * RANK), F32),
            pltpu.SMEM((LD,), jnp.int32),
            pltpu.SMEM((C1,), jnp.int32),
            pltpu.SemaphoreType.DMA((6,)),
        ],
    )
    before = linear_shift(pay, 1)
    after = linear_shift(pay, -1)
    received = lax.all_to_all(send, "sub", 0, 0)
    cl_own, top_send = call(
        middle_kernel,
        [base],
        [],
        [received, cluster_skeleton, top_skeleton],
        [((C1 * 8 + 24, TILE), F32), ((leaf_count, 1, 10 * TILE), F32)],
        [],
        loose=[before, after],
    )
    top_all = lax.all_to_all(top_send, "leaf", 0, 0, tiled=True)
    cl_before = leaf_shift(cl_own, 1)
    cl_after = leaf_shift(cl_own, -1)

    near_sum, far_sum, inverse = call(
        interaction_kernel,
        [base],
        [morton_order, near_list, far_leaf],
        [pay, before, after],
        [((COLS, PTS), F32), ((COLS, PTS), F32), ((16, TILE), jnp.int32)],
        [
            pltpu.VMEM((2 * RN + LD + 1, 8, TILE), F32),
            pltpu.VMEM((2 * RN + LD + 1, LEAF, 32), BF16),
            pltpu.VMEM((3 * LD, 8, TILE), F32),
            pltpu.VMEM((3 * LD, LEAF, 32), BF16),
            pltpu.VMEM((LD, LEAF, 8), F32),
            pltpu.VMEM((PTS, 32), F32),
            pltpu.VMEM((PTS, 32), F32),
            pltpu.VMEM((1, PTS), jnp.int32),
            pltpu.SMEM((LD, NB), jnp.int32),
            pltpu.SMEM((LD, F0), jnp.int32),
            pltpu.SemaphoreType.DMA((3,)),
        ],
        flops=20 * 7_000_000,
        trans=7_000_000,
    )
    (z1,) = call(
        cluster_kernel,
        [base],
        [far_cluster],
        [cl_own, cl_before, cl_after],
        [((C1 // SUB * 8, TILE), F32)],
        [
            pltpu.VMEM((3 * C1, 8, TILE), F32),
            pltpu.VMEM((3 * C1, LEAF, 32), BF16),
            pltpu.VMEM((C1 // SUB * LEAF, 32), F32),
            pltpu.SMEM((C1, F1), jnp.int32),
            pltpu.SemaphoreType.DMA((1,)),
        ],
        flops=20 * 262_144,
        trans=262_144,
        loose=[near_sum],
    )
    (share,) = call(
        top_kernel,
        [base],
        [top_counts, far_top, top_skeleton],
        [top_all, z1],
        [(((C2 + C1 // SUB) * 8, TILE), F32)],
        [
            pltpu.VMEM((C2 * LEAF, 32), F32),
            pltpu.SMEM((C2, MAXF2), jnp.int32),
            pltpu.SMEM(top_counts.shape, jnp.int32),
            pltpu.SMEM((8, MAXF2), jnp.int32),
            pltpu.VMEM((C2, 3 * RANK), F32),
            pltpu.SemaphoreType.DMA((3,)),
        ],
    )
    group = lax.all_to_all(
        jnp.broadcast_to(share, (SUB, (C2 + C1 // SUB) * 8, TILE)), "sub", 0, 0
    )
    (product,) = call(
        downward_kernel,
        [base],
        [leaf_parent, cluster_parent],
        [group, near_sum, far_sum, inverse, basis, transfer, cluster_trans],
        [((COLS, PTS), F32)],
        [
            pltpu.VMEM((C2, COLS, RANK), F32),
            pltpu.VMEM((C1, COLS, RANK), F32),
            pltpu.VMEM((COLS, PTS), F32),
            pltpu.SMEM((LD,), jnp.int32),
            pltpu.SMEM((C1,), jnp.int32),
            pltpu.SemaphoreType.DMA((2,)),
        ],
    )
    return product


def solution(mesh):
    both = ("leaf", "sub")
    placed = (
        P(None, both), P(both, None), P(None, both), P(both, None), P(both, None), P(both, None),
        P(both, None), P(both, None), P(both), P("leaf", None), P("leaf", None), P("leaf", None),
        P("leaf"), P("leaf", None), P(), P(),
    )
    return jax.shard_map(
        local, mesh=mesh, in_specs=placed, out_specs=P(None, both), check_vma=False
    )
```

time: 143 us -> 109 us (0.76)
  the two profiles are of different devices: /device:TPU:118 before, /device:TPU:150 now
where the time goes in v1:
time: 109 us; the launch traced here: 108 us
  Pallas kernels  47.1 us (43%)
  starting transfers between devices  33.1 us (30%)
  blocking collectives  18.8 us (17%)
  local copies, waits for them, and re-layouts  9.04 us (8%)
    pallas_call x6, Pallas kernels, call(): pl.pallas_call(body, in_specs=[SMEM] * len(scalars) + [ANY] * (len(loose)...  47.1 us
    all_to_all x1, starting transfers between devices, local(): top_all = lax.all_to_all(top_send, 'leaf', 0, 0, tiled=True)  20.3 us
    all_to_all x1, blocking collectives, local(): received = lax.all_to_all(send, 'sub', 0, 0)  11.8 us
    ppermute x2, starting transfers between devices, leaf_shift(): return lax.ppermute(value, 'leaf', pairs)  7.96 us
    all_to_all x1, blocking collectives, local(): lax.all_to_all(jnp.broadcast_to(share, (SUB, (C2 + C1 // SUB) * 8, TILE))...  7.02 us
    unnamed x35, local copies, waits for them, and re-layouts  7.01 us
    ppermute x2, starting transfers between devices, linear_shift(): return lax.ppermute(value, ('leaf', 'sub'), pairs)  4.82 us
  transfers between devices with their start and end apart: 5, of which 0 were waited for; matrix products, arithmetic and copies ran while one was open for 1% of the time, Pallas kernels for 23%

profile of v1, /device:TPU:150, one launch (start us, length us, event | category | flops | bytes accessed | tf_op | source)
XLA Modules:
  0.0 108.3 jit_solution(11160451278501597659)
XLA Ops:
  0.0 1.2 %reshape.11.cluster_transfer_ref = f32[16,64,64]{2,1,0:T(8,128)S(1)} reshape(f32[16,4096]{1,0:T(8,128)} %param.27) | data formatting | bytes 524288 | tf_op jit(solution)/shard_map/reshape | solution.py:512
  1.2 0.4 reshape.9.basis_ref
  1.7 0.6 copy-done.15
  2.8 3.1 %shard_map.154 = (f32[40,2048]{1,0:T(8,128)S(1)}, f32[4,136,128]{2,1,0:T(8,128)S(1)}) custom-call(s32[4]{0:T(128)S(1)} %pad_add_fusion.base, f32[16,2048]{1,0:T(8,128)} %x_any.1, s32[1,2048]{1,0:T(1,128)} %order_any.3, f32[3,2048]{1,0:T(4,128)} %points_any.1, f32[32,192]{1,0:T(8,128)} %skel_any.1, s32[32]{0:T(128)} %leaf_any.3, s32[16]{0:T(128)} %cluster_any.5, ...), custom_call_target="tpu_custom_call" | custom-call | bytes 4194304 | tf_op jit(solution)/shard_map/pallas_call | solution.py:477
  5.9 2.9 %collective-permute-start.1 = (f32[40,2048]{1,0:T(8,128)S(1)}, f32[40,2048]{1,0:T(8,128)S(1)}, u32[]{:S(2)}, u32[]{:S(2)}) collective-permute-start(f32[40,2048]{1,0:T(8,128)S(1)} %get-tuple-element.12.own_ref), channel_id=1, source_target_pairs={{1,0},{2,1},{3,2},{4,3},{5,4},{6,5},{7,6},{8,7},{9,8},{10,9},{11,1... | collective-permute-start | bytes 983048 | tf_op jit(solution)/shard_map/ppermute | solution.py:491
  8.8 1.9 %collective-permute-start = (f32[40,2048]{1,0:T(8,128)S(1)}, f32[40,2048]{1,0:T(8,128)S(1)}, u32[]{:S(2)}, u32[]{:S(2)}) collective-permute-start(f32[40,2048]{1,0:T(8,128)S(1)} %get-tuple-element.12.own_ref), channel_id=1, source_target_pairs={{0,1},{1,2},{2,3},{3,4},{4,5},{5,6},{6,7},{7,8},{8,9},{9,10},{10,1... | collective-permute-start | bytes 983048 | tf_op jit(solution)/shard_map/ppermute | solution.py:491
  10.8 11.8 %all_to_all.15.received_ref = f32[4,136,128]{2,1,0:T(8,128)S(1)} all-to-all(f32[4,136,128]{2,1,0:T(8,128)S(1)} %get-tuple-element.13), channel_id=1, replica_groups=mesh['leaf'=128,'sub'=4] {'sub'}, dimensions={0} | all-to-all | bytes 557056 | tf_op jit(solution)/shard_map/all_to_all | solution.py:534
  22.6 1.3 %shard_map.155 = (f32[152,128]{1,0:T(8,128)}, f32[128,1,1280]{2,1,0:T(1,128)S(1)}) custom-call(s32[4]{0:T(128)S(1)} %pad_add_fusion.base, f32[40,2048]{1,0:T(8,128)S(1)} %collective-permute-done.before_any.before_ref, f32[40,2048]{1,0:T(8,128)S(1)} %collective-permute-done.1.after_any.after_ref, f32[4,136,128]{2,1,0:T(8,128)S(1)} %all_to_all.15.received_ref, ...), custom_call_target="tpu_custom_call" | custom-call | bytes 4194304 | tf_op jit(solution)/shard_map/pallas_call | solution.py:477
  23.9 0.9 copy-done
  24.7 20.3 %all-to-all-start.1 = ((f32[128,1,1280]{2,1,0:T(1,128)}), f32[128,1,1280]{2,1,0:T(1,128)S(1)}, u32[]{:S(2)}, u32[]{:S(2)}) async-start(f32[128,1,1280]{2,1,0:T(1,128)} %copy-done), calls=%async_computation.1 | async-start | bytes 1310720 | tf_op jit(solution)/shard_map/all_to_all | solution.py:544
  45.1 2.8 %collective-permute-start.3 = (f32[152,128]{1,0:T(8,128)}, f32[152,128]{1,0:T(8,128)}, u32[]{:S(2)}, u32[]{:S(2)}) collective-permute-start(f32[152,128]{1,0:T(8,128)} %get-tuple-element.16.own_ref), channel_id=1, source_target_pairs={{4,0},{8,4},{12,8},{16,12},{20,16},{24,20},{28,24},{32,28},{36,32}... | collective-permute-start | bytes 233480 | tf_op jit(solution)/shard_map/ppermute | solution.py:497
  47.8 5.2 %collective-permute-start.2 = (f32[152,128]{1,0:T(8,128)}, f32[152,128]{1,0:T(8,128)}, u32[]{:S(2)}, u32[]{:S(2)}) collective-permute-start(f32[152,128]{1,0:T(8,128)} %get-tuple-element.16.own_ref), channel_id=1, source_target_pairs={{0,4},{4,8},{8,12},{12,16},{16,20},{20,24},{24,28},{28,32},{32,36}... | collective-permute-start | bytes 233480 | tf_op jit(solution)/shard_map/ppermute | solution.py:497
  53.0 0.7 copy.17.far_any
  53.7 1.0 copy-done.2
  54.7 1.0 copy-done.4
  55.7 1.0 copy-done.13
  56.6 22.1 %shard_map.156 = (f32[16,2048]{1,0:T(8,128)S(1)}, f32[16,2048]{1,0:T(8,128)S(1)}, s32[16,128]{1,0:T(8,128)S(1)}) custom-call(s32[4]{0:T(128)S(1)} %pad_add_fusion.base, s32[1,2048]{1,0:T(1,128)} %order_any.3, s32[32,27]{1,0:T(8,128)} %near_any.1, s32[32,24]{1,0:T(8,128)} %copy.17.far_any, f32[40,2048]{1,0:T(8,128)S(1)} %copy-done.13, ...), custom_call_target="tpu_custom_call" | custom-call | flops 140000000 | bytes 4194304 | tf_op jit(solution)/shard_map/pallas_call | solution.py:477
  78.8 0.6 copy-done.10
  79.4 0.7 copy-done.8
  80.0 3.1 %shard_map.157.z1_ref = f32[32,128]{1,0:T(8,128)S(1)} custom-call(s32[4]{0:T(128)S(1)} %copy-done.8, f32[16,2048]{1,0:T(8,128)S(1)} %get-tuple-element.15.near_any.near_ref, s32[16,16]{1,0:T(8,128)} %cluster_any.4, f32[152,128]{1,0:T(8,128)} %get-tuple-element.16.own_ref, f32[152,128]{1,0:T(8,128)} %collective-permute-done.2.before_ref, ...), custom_call_target="tpu_custom_call" | custom-call | flops 5242880 | bytes 4194304 | tf_op jit(solution)/shard_map/pallas_call | solution.py:477
  83.2 0.7 copy-done.9
  83.8 13.7 %shard_map.158 = f32[64,128]{1,0:T(8,128)S(1)} custom-call(s32[4]{0:T(128)S(1)} %copy-done.9, s32[512]{0:T(512)} %counts_any.1, s32[512,128]{1,0:T(8,128)} %table_any.1, f32[4,192]{1,0:T(4,128)} %target_any.1, f32[128,1,1280]{2,1,0:T(1,128)S(1)} %all-to-all-done.1.source_ref, f32[32,128]{1,0:T(8,128)S(1)} %shard_map.157.z1_ref), custom_call_target="tpu_custom_call" | custom-call | bytes 4194304 | tf_op jit(solution)/shard_map/pallas_call | solution.py:477
  97.5 7.0 %all_to_all.16.group_ref = f32[4,64,128]{2,1,0:T(8,128)S(1)} all-to-all(f32[4,64,128]{2,1,0:T(8,128)S(1)} %broadcast_in_dim.3), channel_id=1, replica_groups=mesh['leaf'=128,'sub'=4] {'sub'}, dimensions={0} | all-to-all | bytes 262144 | tf_op jit(solution)/shard_map/all_to_all | solution.py:602
  104.5 3.8 %shard_map.159 = f32[16,2048]{1,0:T(8,128)} custom-call(s32[4]{0:T(128)S(1)} %copy-done.9, s32[32]{0:T(128)} %leaf_any.3, s32[16]{0:T(128)} %cluster_any.5, f32[4,64,128]{2,1,0:T(8,128)S(1)} %all_to_all.16.group_ref, f32[16,2048]{1,0:T(8,128)S(1)} %get-tuple-element.15.near_any.near_ref, f32[16,2048]{1,0:T(8,128)S(1)} %get-tuple-element.17.far_ref, ...), custom_call_target="tpu_custom_call" | custom-call | bytes 4194304 | tf_op jit(solution)/shard_map/pallas_call | solution.py:477
  (34 shorter events, 0.6 us)
Async XLA Ops:
  0.0 1.2 %copy-start.14 = (f32[32,4096]{1,0:T(8,128)S(1)}, f32[32,4096]{1,0:T(8,128)}, u32[]{:S(2)}) copy-start(f32[32,4096]{1,0:T(8,128)} %param.19) | copy-start | bytes 1572868
  1.2 1.0 copy-start.15
  2.8 50.9 %copy-start.7 = (s32[4]{0:T(128)}, s32[4]{0:T(128)S(1)}, u32[]{:S(2)}) copy-start(s32[4]{0:T(128)S(1)} %pad_add_fusion.base) | copy-start | bytes 52
  5.9 16.6 %copy-start.12 = (f32[40,2048]{1,0:T(8,128)}, f32[40,2048]{1,0:T(8,128)S(1)}, u32[]{:S(2)}) copy-start(f32[40,2048]{1,0:T(8,128)S(1)} %get-tuple-element.12.own_ref) | copy-start | bytes 983044
  5.9 16.6 %collective-permute-start.1 = (f32[40,2048]{1,0:T(8,128)S(1)}, f32[40,2048]{1,0:T(8,128)S(1)}, u32[]{:S(2)}, u32[]{:S(2)}) collective-permute-start(f32[40,2048]{1,0:T(8,128)S(1)} %get-tuple-element.12.own_ref), channel_id=1, source_target_pairs={{1,0},{2,1},{3,2},{4,3},{5,4},{6,5},{7,6},{8,7},{9,8},{10,9},{11,1... | collective-permute-start | bytes 983048 | tf_op jit(solution)/shard_map/ppermute | solution.py:491
  8.8 13.7 %collective-permute-start = (f32[40,2048]{1,0:T(8,128)S(1)}, f32[40,2048]{1,0:T(8,128)S(1)}, u32[]{:S(2)}, u32[]{:S(2)}) collective-permute-start(f32[40,2048]{1,0:T(8,128)S(1)} %get-tuple-element.12.own_ref), channel_id=1, source_target_pairs={{0,1},{1,2},{2,3},{3,4},{4,5},{5,6},{6,7},{7,8},{8,9},{9,10},{10,1... | collective-permute-start | bytes 983048 | tf_op jit(solution)/shard_map/ppermute | solution.py:491
  10.7 11.8 %copy-start.5 = (f32[16,192]{1,0:T(8,128)S(1)}, f32[16,192]{1,0:T(8,128)}, u32[]{:S(2)}) copy-start(f32[16,192]{1,0:T(8,128)} %cluster_skel_ref.1) | copy-start | bytes 36868
  10.8 11.8 %copy-start.6 = (f32[4,192]{1,0:T(4,128)S(1)}, f32[4,192]{1,0:T(4,128)}, u32[]{:S(2)}) copy-start(f32[4,192]{1,0:T(4,128)} %target_any.1) | copy-start | bytes 9220
  22.5 1.3 %copy-start.1 = (f32[40,2048]{1,0:T(8,128)}, f32[40,2048]{1,0:T(8,128)S(1)}, u32[]{:S(2)}) copy-start(f32[40,2048]{1,0:T(8,128)S(1)} %collective-permute-done.1.after_any.after_ref) | copy-start | bytes 983044
  22.6 1.3 %copy-start.3 = (f32[40,2048]{1,0:T(8,128)}, f32[40,2048]{1,0:T(8,128)S(1)}, u32[]{:S(2)}) copy-start(f32[40,2048]{1,0:T(8,128)S(1)} %collective-permute-done.before_any.before_ref) | copy-start | bytes 983044
  23.8 0.9 copy-start
  24.7 28.3 %copy-start.16 = (s32[32,24]{0,1:T(8,128)S(1)}, s32[32,24]{0,1:T(8,128)}, u32[]{:S(2)}) copy-start(s32[32,24]{0,1:T(8,128)} %param.21) | copy-start | bytes 9220
  24.7 58.4 %all-to-all-start.1 = ((f32[128,1,1280]{2,1,0:T(1,128)}), f32[128,1,1280]{2,1,0:T(1,128)S(1)}, u32[]{:S(2)}, u32[]{:S(2)}) async-start(f32[128,1,1280]{2,1,0:T(1,128)} %copy-done), calls=%async_computation.1 | async-start | bytes 1310720 | tf_op jit(solution)/shard_map/all_to_all | solution.py:544
  45.1 34.3 %collective-permute-start.3 = (f32[152,128]{1,0:T(8,128)}, f32[152,128]{1,0:T(8,128)}, u32[]{:S(2)}, u32[]{:S(2)}) collective-permute-start(f32[152,128]{1,0:T(8,128)} %get-tuple-element.16.own_ref), channel_id=1, source_target_pairs={{4,0},{8,4},{12,8},{16,12},{20,16},{24,20},{28,24},{32,28},{36,32}... | collective-permute-start | bytes 233480 | tf_op jit(solution)/shard_map/ppermute | solution.py:497
  47.8 31.6 %collective-permute-start.2 = (f32[152,128]{1,0:T(8,128)}, f32[152,128]{1,0:T(8,128)}, u32[]{:S(2)}, u32[]{:S(2)}) collective-permute-start(f32[152,128]{1,0:T(8,128)} %get-tuple-element.16.own_ref), channel_id=1, source_target_pairs={{0,4},{4,8},{8,12},{12,16},{16,20},{20,24},{24,28},{28,32},{32,36}... | collective-permute-start | bytes 233480 | tf_op jit(solution)/shard_map/ppermute | solution.py:497
  53.7 1.0 copy-start.2
  54.7 1.0 copy-start.4
  55.7 1.0 copy-start.13
  78.8 0.6 copy-start.10
  79.4 0.7 copy-start.8
  83.2 0.7 copy-start.9
  97.5 7.0 %copy-start.11 = (s32[16,128]{1,0:T(8,128)S(1)}, s32[16,128]{1,0:T(8,128)}, u32[]{:S(2)}) copy-start(s32[16,128]{1,0:T(8,128)} %copy-done.10) | copy-start | bytes 24580

commit v2 on v1

--- a/solution.py
+++ b/solution.py
@@ -237,9 +237,15 @@
 
 def stage_pair(pay, row_value, row_place, tile, place_ref, weight_ref, slot):
     lanes = slice(tile * TILE, (tile + 1) * TILE)
-    weights = weights_of(pay[row_value : row_value + 16, lanes])
-    weight_ref[slot] = weights[:LEAF]
-    weight_ref[slot + 1] = weights[LEAF:]
+    values = pay[row_value : row_value + 16, lanes]
+    high = values.astype(BF16).astype(F32)
+    both = jnp.concatenate([high, values - high], axis=0)
+    turned = pltpu.roll(both, RANK, 1)
+    left = lax.broadcasted_iota(jnp.int32, (32, TILE), 1) < RANK
+    weight_ref[slot, 0] = jnp.where(left, both, 0.0).astype(BF16)
+    weight_ref[slot, 1] = jnp.where(left, 0.0, turned).astype(BF16)
+    weight_ref[slot + 1, 0] = jnp.where(left, turned, 0.0).astype(BF16)
+    weight_ref[slot + 1, 1] = jnp.where(left, 0.0, both).astype(BF16)
     place = pay[row_place : row_place + 3, lanes]
     swapped = pltpu.roll(place, RANK, 1)
     lane = lax.broadcasted_iota(jnp.int32, (3, TILE), 1)
@@ -253,14 +259,35 @@
         write(pair, (block[:16] + block[16:]) * INV_FOUR_PI)
 
 
+def quad_blocks(target, group, place_ref, weight_ref):
+    high, low, weights = [], [], []
+    for first, second in ((group[0], group[1]), (group[2], group[3])):
+        source = source_pair(place_ref[first], place_ref[second])
+        highs, lows = [], []
+        for chunk in range(LEAF // 16):
+            at = slice(chunk * 16, chunk * 16 + 16)
+            block_high, block_low = split(green([axis[at] for axis in target], source))
+            highs.append(block_high)
+            lows.append(block_low)
+        high.append(jnp.concatenate(highs, axis=0))
+        low.append(jnp.concatenate(lows, axis=0))
+        weights.append(weight_ref[first, 0] + weight_ref[second, 1])
+    return joined(high), joined(low), joined(weights)
+
+
 def interaction_kernel(
-    base, order_any, near_any, far_any, own_ref, before_ref, after_ref,
-    near_ref, far_ref, inverse_ref,
+    base, own_any, before_any, after_any, near_any, far_any,
+    near_ref, far_ref,
     near_place, near_weight, far_place, far_weight, target_cols, near_rows, far_rows,
-    order_ref, near_ids, far_ids, sems,
+    own_ref, before_ref, after_ref, near_ids, far_ids, sems,
 ):
-    copies = fetched([order_any, near_any, far_any], [order_ref, near_ids, far_ids], sems)
+    copies = fetched(
+        [own_any, before_any, after_any, near_any, far_any],
+        [own_ref, before_ref, after_ref, near_ids, far_ids],
+        sems,
+    )
     tiles = PTS // TILE
+    copies[0].wait()
     for tile in range(tiles):
         stage_pair(own_ref, 0, 32, tile, near_place, near_weight, RN + 2 * tile)
         stage_pair(own_ref, 16, 35, tile, far_place, far_weight, LD + 2 * tile)
@@ -268,7 +295,7 @@
         block = own_ref[32:40, tile * TILE : (tile + 1) * TILE].T
         target_cols[2 * tile] = block[:LEAF]
         target_cols[2 * tile + 1] = block[LEAF:]
-    for copy in copies:
+    for copy in copies[1:]:
         copy.wait()
     for tile in range(tiles // 2):
         stage_pair(before_ref, 0, 32, tiles // 2 + tile, near_place, near_weight, 2 * tile)
@@ -276,40 +303,56 @@
     for tile in range(tiles):
         stage_pair(before_ref, 16, 35, tile, far_place, far_weight, 2 * tile)
         stage_pair(after_ref, 16, 35, tile, far_place, far_weight, 2 * LD + 2 * tile)
-    near_weight[2 * RN + LD] = jnp.zeros((LEAF, 32), BF16)
-    near_place[2 * RN + LD, 0:3] = jnp.zeros((3, TILE), F32)
-
-    def leaf_step(leaf, carry):
-        columns = target_cols[leaf]
-        target = spread(columns)
-        ids = [near_ids[leaf, k] - base[2] + RN for k in range(NB)] + [2 * RN + LD]
-        near_rows[pl.ds(leaf * LEAF, LEAF), :] = listed_product(target, ids, near_place, near_weight)
-        target = spread(columns[:, 3:6])
-        ids = [far_ids[leaf, k] - base[2] + RF for k in range(F0)]
-        far_rows[pl.ds(leaf * LEAF, LEAF), :] = listed_product(target, ids, far_place, far_weight)
-        return carry
-
-    lax.fori_loop(0, LD, leaf_step, 0, unroll=2)
-
-    def write_near(pair, block):
-        near_ref[:, pair * TILE : (pair + 1) * TILE] = block
-
-    def write_far(pair, block):
-        far_ref[:, pair * TILE : (pair + 1) * TILE] = block
-
-    finish_rows(near_rows, LD, write_near)
-    finish_rows(far_rows, LD, write_far)
-
-    order = order_ref[...]
-    position = lax.broadcasted_iota(jnp.int32, (16, PTS), 1)
-    hit = (order >> 7) == lax.broadcasted_iota(jnp.int32, (16, PTS), 0)
-    coarse = jnp.where(hit, (position >> 7).astype(F32), 0.0)
-    fine = jnp.where(hit, (position & (TILE - 1)).astype(F32), 0.0)
-    lhs = jnp.concatenate([coarse, fine], axis=0).astype(BF16)
-    lane_of = (order & (TILE - 1)) == lax.broadcasted_iota(jnp.int32, (TILE, PTS), 0)
-    rhs = jnp.where(lane_of, 1.0, 0.0).astype(BF16)
-    found = lax.dot_general(lhs, rhs, (((1,), (1,)), ((), ())), preferred_element_type=F32)
-    inverse_ref[...] = found[:16].astype(jnp.int32) * TILE + found[16:].astype(jnp.int32)
+    for ref, slot in ((near_place, 2 * RN + LD), (far_place, 3 * LD)):
+        ref[slot, 0:3] = jnp.zeros((3, TILE), F32)
+    for ref, slot in ((near_weight, 2 * RN + LD), (far_weight, 3 * LD)):
+        ref[slot] = jnp.zeros((2, 32, TILE), BF16)
+
+    def leaf_pair(accs):
+        def leaf_step(pair, carry):
+            for unit in range(2):
+                leaf = 2 * pair + unit
+                columns = target_cols[leaf]
+                near_target, far_target = spread(columns), spread(columns[:, 3:6])
+                near = [near_ids[leaf, k] - base[2] + RN for k in range(NB)] + [2 * RN + LD]
+                far = [far_ids[leaf, k] - base[2] + RF for k in range(F0)]
+                for quad in range(len(near) // 4):
+                    part = slice(4 * quad, 4 * quad + 4)
+                    high, low, weights = quad_blocks(near_target, near[part], near_place, near_weight)
+                    if quad < F0 // 4:
+                        far_high, far_low, far_weights = quad_blocks(
+                            far_target, far[part], far_place, far_weight
+                        )
+                    else:
+                        far_high = far_low = jnp.zeros((LEAF, 2 * TILE), BF16)
+                        far_weights = jnp.zeros((32, 2 * TILE), BF16)
+                    block = jnp.concatenate([high, low, far_high, far_low], axis=0)
+                    pltpu.matmul_push_rhs(block, quad % 2, unit, transpose=True)
+                    pltpu.matmul_acc_lhs(
+                        accs[unit], jnp.concatenate([weights, far_weights], axis=0), quad % 2
+                    )
+            for unit in range(2):
+                total = pltpu.matmul_pop(accs[unit])
+                for rows_ref, part in (
+                    (near_rows, total[:32, :TILE]), (far_rows, total[32:, TILE:])
+                ):
+                    rows_ref[2 * pair + unit] = part[:COLS] + part[COLS:]
+            return carry
+
+        lax.fori_loop(0, LD // 2, leaf_step, 0, unroll=4)
+
+    pl.run_scoped(
+        lambda first, second: leaf_pair((first, second)),
+        pltpu.ACC(0)((LEAF, 2 * TILE), F32),
+        pltpu.ACC(1)((LEAF, 2 * TILE), F32),
+    )
+    left = lax.broadcasted_iota(jnp.int32, (COLS, TILE), 1) < RANK
+    for rows_ref, out_ref in ((near_rows, near_ref), (far_rows, far_ref)):
+        for pair in range(LD // 2):
+            first, second = rows_ref[2 * pair], rows_ref[2 * pair + 1]
+            first = first + pltpu.roll(first, RANK, 1)
+            second = second + pltpu.roll(second, RANK, 1)
+            out_ref[:, pair * TILE : (pair + 1) * TILE] = jnp.where(left, first, second) * INV_FOUR_PI
 
 
 def write_tiles(rows_ref, count, out_ref, start):
@@ -322,11 +365,11 @@
 
 
 def cluster_kernel(
-    base, near_any, cluster_any, own_ref, before_ref, after_ref,
-    z1_ref, cl_place, cl_weight, cl_rows, cluster_ids, sems,
+    base, near_any, cluster_any, order_any, own_ref, before_ref, after_ref,
+    z1_ref, inverse_ref, cl_place, cl_weight, cl_rows, cluster_ids, order_ref, sems,
 ):
     del near_any
-    copies = fetched([cluster_any], [cluster_ids], sems)
+    copies = fetched([cluster_any, order_any], [cluster_ids, order_ref], sems)
     for part, ref in enumerate((before_ref, own_ref, after_ref)):
         for cluster in range(C1):
             tile = ref[cluster * 8 : cluster * 8 + 8, :]
@@ -355,10 +398,21 @@
     lax.fori_loop(0, C1 // SUB, cluster_step, 0, unroll=2)
     write_tiles(cl_rows, C1 // SUB, z1_ref, 0)
 
+    order = order_ref[...]
+    position = lax.broadcasted_iota(jnp.int32, (16, PTS), 1)
+    hit = (order >> 7) == lax.broadcasted_iota(jnp.int32, (16, PTS), 0)
+    coarse = jnp.where(hit, (position >> 7).astype(F32), 0.0)
+    fine = jnp.where(hit, (position & (TILE - 1)).astype(F32), 0.0)
+    lhs = jnp.concatenate([coarse, fine], axis=0).astype(BF16)
+    lane_of = (order & (TILE - 1)) == lax.broadcasted_iota(jnp.int32, (TILE, PTS), 0)
+    rhs = jnp.where(lane_of, 1.0, 0.0).astype(BF16)
+    found = lax.dot_general(lhs, rhs, (((1,), (1,)), ((), ())), preferred_element_type=F32)
+    inverse_ref[...] = found[:16].astype(jnp.int32) * TILE + found[16:].astype(jnp.int32)
+
 
 def top_kernel(
     base, counts_any, table_any, target_any, source_ref, z1_ref,
-    out_ref, rows, lists, top_counts, table, target_ref, sems,
+    out_ref, rows, spread_ref, order, lists, top_counts, table, target_ref, sems,
 ):
     aligned = pl.multiple_of(base[1] // 8 * 8, 8)
     copies = fetched(
@@ -367,57 +421,94 @@
     out_ref[C2 * 8 :, :] = z1_ref[...]
     for copy in copies:
         copy.wait()
-    def scan(top):
-        def note(slot, found):
+    lane = lax.broadcasted_iota(jnp.int32, (8, TILE), 1)
+    left = lane < RANK
+    items = 0
+    for top in range(C2):
+
+        def note(slot, found, top=top):
             cluster = table[base[1] - aligned + top, slot]
             lists[top, found] = cluster // SUB
             return found + jnp.where(cluster % SUB == base[3], 1, 0)
 
-        return lax.fori_loop(0, top_counts[base[1] + top], note, 0)
-
-    for top in range(C2):
-        found = scan(top)
+        found = lax.fori_loop(0, top_counts[base[1] + top], note, 0)
+        for k in range(GROUP):
+            lists[top, found + k] = -1
+        first_item = items
+
+        def plan(quad, count, top=top, first_item=first_item):
+            order[first_item + quad] = top * (2 * MAXF2) + GROUP * quad
+            return count + 1
+
+        items = lax.fori_loop(0, (found + GROUP - 1) // GROUP, plan, items)
         skel = jnp.concatenate(
             [target_ref[top : top + 1, k * RANK : (k + 1) * RANK] for k in range(3)]
             + [jnp.zeros((5, RANK), F32)],
             axis=0,
         )
         columns = joined([skel, jnp.zeros((8, RANK), F32)]).T
-        target = spread(columns[:LEAF])
-        where = slice(top * LEAF, (top + 1) * LEAF)
-        rows[where, :] = jnp.zeros((LEAF, 32), F32)
-
-        def step(quad, carry, target=target, found=found, where=where, top=top):
-            places, weights = [], []
-            lane = lax.broadcasted_iota(jnp.int32, (1, TILE), 1)
-            for k in range(GROUP):
-                at = GROUP * quad + k
-                live = at < found
-                source = jnp.where(live, lists[top, jnp.where(live, at, 0)], 0)
-                tile = jnp.concatenate(
-                    [source_ref[source, :, j * TILE : (j + 1) * TILE] for j in range(8)], axis=0
-                )
-                weights.append(weights_of(from_tile(tile) * jnp.where(live, 1.0, 0.0).astype(F32)))
-                first = source_ref[source, :, 8 * TILE : 9 * TILE]
-                second = source_ref[source, :, 9 * TILE : 10 * TILE]
-                places.append((first, second))
-            high, low = [], []
-            for (a0, a1), (b0, b1) in ((places[0], places[1]), (places[2], places[3])):
-                rows_of = [
-                    jnp.where(lane < RANK, a0, pltpu.roll(b0, RANK, 1)),
-                    jnp.where(lane < RANK, pltpu.roll(a0, RANK, 1), b0),
-                    jnp.where(lane < RANK, a1, pltpu.roll(b1, RANK, 1)),
-                ]
-                block_high, block_low = split(green(target, jnp.concatenate(rows_of, axis=0)))
-                high.append(block_high)
-                low.append(block_low)
-            lhs = jnp.concatenate([joined(high), joined(low)], axis=0)
-            part = jnp.dot(lhs, jnp.concatenate(weights, axis=0), preferred_element_type=F32)
-            rows[where, :] = rows[where, :] + part[:LEAF] + part[LEAF:]
-            return carry
-
-        lax.fori_loop(0, (found + GROUP - 1) // GROUP, step, 0)
-    write_tiles(rows, C2, out_ref, 0)
+        for k, axis in enumerate(spread(columns[:LEAF])):
+            spread_ref[top, k] = axis
+        rows[top] = jnp.zeros((32, TILE), F32)
+    for k in range(GROUP):
+        lists[C2, k] = -1
+    order[items] = C2 * (2 * MAXF2)
+
+    def product(item):
+        top, start = item // (2 * MAXF2), item % (2 * MAXF2)
+        target = jnp.minimum(top, C2 - 1)
+        axes = [spread_ref[target, k] for k in range(3)]
+        tiles, places = [], []
+        for k in range(GROUP):
+            listed = lists[top, start + k]
+            source = jnp.maximum(listed, 0)
+            keep = jnp.where(listed >= 0, 1.0, 0.0).astype(F32)
+            tile = jnp.concatenate(
+                [source_ref[source, :, j * TILE : (j + 1) * TILE] for j in range(8)], axis=0
+            )
+            tiles.append(tile * keep)
+            places.append(
+                (source_ref[source, :, 8 * TILE : 9 * TILE], source_ref[source, :, 9 * TILE : 10 * TILE])
+            )
+        high, low, weights = [], [], []
+        one = left[:1]
+        for first in (0, 2):
+            a, b = tiles[first], tiles[first + 1]
+            values = jnp.concatenate(
+                [jnp.where(left, a, pltpu.roll(b, RANK, 1)), jnp.where(left, pltpu.roll(a, RANK, 1), b)],
+                axis=0,
+            )
+            weights.append(jnp.concatenate(split(values), axis=0))
+            (a0, a1), (b0, b1) = places[first], places[first + 1]
+            source = jnp.concatenate(
+                [
+                    jnp.where(one, a0, pltpu.roll(b0, RANK, 1)),
+                    jnp.where(one, pltpu.roll(a0, RANK, 1), b0),
+                    jnp.where(one, a1, pltpu.roll(b1, RANK, 1)),
+                ],
+                axis=0,
+            )
+            block_high, block_low = split(green(axes, source))
+            high.append(block_high)
+            low.append(block_low)
+        blocks = jnp.concatenate([joined(high), joined(low)], axis=0)
+        part = lax.dot_general(
+            joined(weights), blocks, (((1,), (1,)), ((), ())), preferred_element_type=F32
+        )
+        return target, part
+
+    def step(pair, carry):
+        parts = [product(order[2 * pair + k]) for k in range(2)]
+        for target, part in parts:
+            rows[target] = rows[target] + part
+        return carry
+
+    lax.fori_loop(0, (items + 1) // 2, step, 0)
+    for top in range(C2):
+        total = rows[top]
+        total = total[:COLS] + total[COLS:]
+        total = (total + pltpu.roll(total, RANK, 1)) * INV_FOUR_PI
+        out_ref[top * 8 : top * 8 + 8, :] = jnp.where(left, total[:8], total[8:])
 
 
 def downward_kernel(
@@ -545,40 +636,43 @@
     cl_before = leaf_shift(cl_own, 1)
     cl_after = leaf_shift(cl_own, -1)
 
-    near_sum, far_sum, inverse = call(
+    near_sum, far_sum = call(
         interaction_kernel,
         [base],
-        [morton_order, near_list, far_leaf],
-        [pay, before, after],
-        [((COLS, PTS), F32), ((COLS, PTS), F32), ((16, TILE), jnp.int32)],
+        [pay, before, after, near_list, far_leaf],
+        [],
+        [((COLS, PTS), F32), ((COLS, PTS), F32)],
         [
             pltpu.VMEM((2 * RN + LD + 1, 8, TILE), F32),
-            pltpu.VMEM((2 * RN + LD + 1, LEAF, 32), BF16),
-            pltpu.VMEM((3 * LD, 8, TILE), F32),
-            pltpu.VMEM((3 * LD, LEAF, 32), BF16),
+            pltpu.VMEM((2 * RN + LD + 1, 2, 32, TILE), BF16),
+            pltpu.VMEM((3 * LD + 1, 8, TILE), F32),
+            pltpu.VMEM((3 * LD + 1, 2, 32, TILE), BF16),
             pltpu.VMEM((LD, LEAF, 8), F32),
-            pltpu.VMEM((PTS, 32), F32),
-            pltpu.VMEM((PTS, 32), F32),
-            pltpu.VMEM((1, PTS), jnp.int32),
+            pltpu.VMEM((LD, COLS, TILE), F32),
+            pltpu.VMEM((LD, COLS, TILE), F32),
+            pltpu.VMEM((ROWS, PTS), F32),
+            pltpu.VMEM((ROWS, PTS), F32),
+            pltpu.VMEM((ROWS, PTS), F32),
             pltpu.SMEM((LD, NB), jnp.int32),
             pltpu.SMEM((LD, F0), jnp.int32),
-            pltpu.SemaphoreType.DMA((3,)),
+            pltpu.SemaphoreType.DMA((5,)),
         ],
         flops=20 * 7_000_000,
         trans=7_000_000,
     )
-    (z1,) = call(
+    z1, inverse = call(
         cluster_kernel,
         [base],
-        [far_cluster],
+        [far_cluster, morton_order],
         [cl_own, cl_before, cl_after],
-        [((C1 // SUB * 8, TILE), F32)],
+        [((C1 // SUB * 8, TILE), F32), ((16, TILE), jnp.int32)],
         [
             pltpu.VMEM((3 * C1, 8, TILE), F32),
             pltpu.VMEM((3 * C1, LEAF, 32), BF16),
             pltpu.VMEM((C1 // SUB * LEAF, 32), F32),
             pltpu.SMEM((C1, F1), jnp.int32),
-            pltpu.SemaphoreType.DMA((1,)),
+            pltpu.VMEM((1, PTS), jnp.int32),
+            pltpu.SemaphoreType.DMA((2,)),
         ],
         flops=20 * 262_144,
         trans=262_144,
@@ -591,8 +685,10 @@
         [top_all, z1],
         [(((C2 + C1 // SUB) * 8, TILE), F32)],
         [
-            pltpu.VMEM((C2 * LEAF, 32), F32),
-            pltpu.SMEM((C2, MAXF2), jnp.int32),
+            pltpu.VMEM((C2, 32, TILE), F32),
+            pltpu.VMEM((C2, 3, LEAF, TILE), F32),
+            pltpu.SMEM((C2 * MAXF2 // GROUP + 8,), jnp.int32),
+            pltpu.SMEM((C2 + 1, 2 * MAXF2), jnp.int32),
             pltpu.SMEM(top_counts.shape, jnp.int32),
             pltpu.SMEM((8, MAXF2), jnp.int32),
             pltpu.VMEM((C2, 3 * RANK), F32),

time: 109 us -> 107 us (0.982)
  the two profiles are of different devices: /device:TPU:150 before, /device:TPU:24 now
where the time goes in v2:
time: 107 us; the launch traced here: 106 us
  Pallas kernels  37.2 us (35%)
  starting transfers between devices  29.4 us (27%)
  blocking collectives  24.2 us (23%)
  waiting for transfers between devices  9.19 us (9%)
  local copies, waits for them, and re-layouts  5.49 us (5%)
    pallas_call x6, Pallas kernels, call(): pl.pallas_call(body, in_specs=[SMEM] * len(scalars) + [ANY] * (len(loose)...  37.2 us
    all_to_all x1, blocking collectives, local(): received = lax.all_to_all(send, 'sub', 0, 0)  18.2 us
    all_to_all x1, starting transfers between devices, local(): top_all = lax.all_to_all(top_send, 'leaf', 0, 0, tiled=True)  16.5 us
    ppermute x2, starting transfers between devices, leaf_shift(): return lax.ppermute(value, 'leaf', pairs)  8.61 us
    ppermute x2, waiting for transfers between devices, leaf_shift(): return lax.ppermute(value, 'leaf', pairs)  6.6 us
    all_to_all x1, blocking collectives, local(): lax.all_to_all(jnp.broadcast_to(share, (SUB, (C2 + C1 // SUB) * 8, TILE))...  6.06 us
    ppermute x2, starting transfers between devices, linear_shift(): return lax.ppermute(value, ('leaf', 'sub'), pairs)  4.33 us
    unnamed x29, local copies, waits for them, and re-layouts  3.46 us
  transfers between devices with their start and end apart: 5, of which 3 were waited for; matrix products, arithmetic and copies ran while one was open for 1% of the time, Pallas kernels for 20%

profile of v2, /device:TPU:24, one launch (start us, length us, event | category | flops | bytes accessed | tf_op | source)
XLA Modules:
  0.0 105.8 jit_solution(8491309012715411471)
XLA Ops:
  0.0 1.2 %reshape.11.cluster_transfer_ref = f32[16,64,64]{2,1,0:T(8,128)S(1)} reshape(f32[16,4096]{1,0:T(8,128)} %param.27) | data formatting | bytes 524288 | tf_op jit(solution)/shard_map/reshape | solution.py:603
  1.2 0.4 reshape.9.basis_ref
  1.7 0.6 copy-done.12
  2.3 0.4 reshape.10.transfer_ref
  2.8 3.1 %shard_map.154 = (f32[40,2048]{1,0:T(8,128)S(1)}, f32[4,136,128]{2,1,0:T(8,128)S(1)}) custom-call(s32[4]{0:T(128)S(1)} %pad_add_fusion.base, f32[16,2048]{1,0:T(8,128)} %x_any.1, s32[1,2048]{1,0:T(1,128)} %order_any.3, f32[3,2048]{1,0:T(4,128)} %points_any.1, f32[32,192]{1,0:T(8,128)} %skel_any.1, s32[32]{0:T(128)} %leaf_any.3, s32[16]{0:T(128)} %cluster_any.5, ...), custom_call_target="tpu_custom_call" | custom-call | bytes 4194304 | tf_op jit(solution)/shard_map/pallas_call | solution.py:568
  5.9 2.1 %collective-permute-start.1 = (f32[40,2048]{1,0:T(8,128)S(1)}, f32[40,2048]{1,0:T(8,128)S(1)}, u32[]{:S(2)}, u32[]{:S(2)}) collective-permute-start(f32[40,2048]{1,0:T(8,128)S(1)} %get-tuple-element.13.own_any), channel_id=1, source_target_pairs={{1,0},{2,1},{3,2},{4,3},{5,4},{6,5},{7,6},{8,7},{9,8},{10,9},{11,1... | collective-permute-start | bytes 983048 | tf_op jit(solution)/shard_map/ppermute | solution.py:582
  8.0 2.2 %collective-permute-start = (f32[40,2048]{1,0:T(8,128)S(1)}, f32[40,2048]{1,0:T(8,128)S(1)}, u32[]{:S(2)}, u32[]{:S(2)}) collective-permute-start(f32[40,2048]{1,0:T(8,128)S(1)} %get-tuple-element.13.own_any), channel_id=1, source_target_pairs={{0,1},{1,2},{2,3},{3,4},{4,5},{5,6},{6,7},{7,8},{8,9},{9,10},{10,1... | collective-permute-start | bytes 983048 | tf_op jit(solution)/shard_map/ppermute | solution.py:582
  10.3 18.2 %all_to_all.15.received_ref = f32[4,136,128]{2,1,0:T(8,128)S(1)} all-to-all(f32[4,136,128]{2,1,0:T(8,128)S(1)} %get-tuple-element.14), channel_id=1, replica_groups=mesh['leaf'=128,'sub'=4] {'sub'}, dimensions={0} | all-to-all | bytes 557056 | tf_op jit(solution)/shard_map/all_to_all | solution.py:625
  28.5 1.3 %shard_map.155 = (f32[152,128]{1,0:T(8,128)}, f32[128,1,1280]{2,1,0:T(1,128)S(1)}) custom-call(s32[4]{0:T(128)S(1)} %pad_add_fusion.base, f32[40,2048]{1,0:T(8,128)S(1)} %collective-permute-done.before_any, f32[40,2048]{1,0:T(8,128)S(1)} %collective-permute-done.1.after_any, f32[4,136,128]{2,1,0:T(8,128)S(1)} %all_to_all.15.received_ref, ...), custom_call_target="tpu_custom_call" | custom-call | bytes 4194304 | tf_op jit(solution)/shard_map/pallas_call | solution.py:568
  29.8 0.9 copy-done
  30.6 16.5 %all-to-all-start.1 = ((f32[128,1,1280]{2,1,0:T(1,128)}), f32[128,1,1280]{2,1,0:T(1,128)S(1)}, u32[]{:S(2)}, u32[]{:S(2)}) async-start(f32[128,1,1280]{2,1,0:T(1,128)} %copy-done), calls=%async_computation.1 | async-start | bytes 1310720 | tf_op jit(solution)/shard_map/all_to_all | solution.py:635
  47.1 6.7 %collective-permute-start.3 = (f32[152,128]{1,0:T(8,128)}, f32[152,128]{1,0:T(8,128)}, u32[]{:S(2)}, u32[]{:S(2)}) collective-permute-start(f32[152,128]{1,0:T(8,128)} %get-tuple-element.17.own_ref), channel_id=1, source_target_pairs={{4,0},{8,4},{12,8},{16,12},{20,16},{24,20},{28,24},{32,28},{36,32}... | collective-permute-start | bytes 233480 | tf_op jit(solution)/shard_map/ppermute | solution.py:588
  53.8 1.9 %collective-permute-start.2 = (f32[152,128]{1,0:T(8,128)}, f32[152,128]{1,0:T(8,128)}, u32[]{:S(2)}, u32[]{:S(2)}) collective-permute-start(f32[152,128]{1,0:T(8,128)} %get-tuple-element.17.own_ref), channel_id=1, source_target_pairs={{0,4},{4,8},{8,12},{12,16},{16,20},{20,24},{24,28},{28,32},{32,36}... | collective-permute-start | bytes 233480 | tf_op jit(solution)/shard_map/ppermute | solution.py:588
  55.7 0.7 copy.17.far_any
  56.4 17.7 %shard_map.156 = (f32[16,2048]{1,0:T(8,128)S(1)}, f32[16,2048]{1,0:T(8,128)S(1)}) custom-call(s32[4]{0:T(128)S(1)} %pad_add_fusion.base, f32[40,2048]{1,0:T(8,128)} %copy-done.10, f32[40,2048]{1,0:T(8,128)} %copy-done.2, f32[40,2048]{1,0:T(8,128)} %copy-done.1, s32[32,27]{1,0:T(8,128)} %near_any.1, s32[32,24]{1,0:T(8,128)} %copy.17.far_any), custom_call_target="tpu_custom_call" | custom-call | flops 140000000 | bytes 4194304 | tf_op jit(solution)/shard_map/pallas_call | solution.py:568
  74.2 0.7 collective-permute-done.3.after_ref
  74.8 6.0 %collective-permute-done.2.before_ref = f32[152,128]{1,0:T(8,128)} collective-permute-done((f32[152,128]{1,0:T(8,128)}, f32[152,128]{1,0:T(8,128)}, u32[]{:S(2)}, u32[]{:S(2)}) %collective-permute-start.2) | collective-permute-done | bytes 77856 | tf_op jit(solution)/shard_map/ppermute | solution.py:588
  80.8 3.2 %shard_map.157 = (f32[32,128]{1,0:T(8,128)S(1)}, s32[16,128]{1,0:T(8,128)S(1)}) custom-call(s32[4]{0:T(128)S(1)} %copy-done.6, f32[16,2048]{1,0:T(8,128)S(1)} %get-tuple-element.16.near_any.near_ref, s32[16,16]{1,0:T(8,128)} %cluster_any.4, s32[1,2048]{1,0:T(1,128)} %order_any.3, f32[152,128]{1,0:T(8,128)} %get-tuple-element.17.own_ref, ...), custom_call_target="tpu_custom_call" | custom-call | flops 5242880 | bytes 4194304 | tf_op jit(solution)/shard_map/pallas_call | solution.py:568
  84.0 0.6 copy-done.8
  84.6 2.6 %all-to-all-done.1.source_ref = f32[128,1,1280]{2,1,0:T(1,128)S(1)} async-done(((f32[128,1,1280]{2,1,0:T(1,128)}), f32[128,1,1280]{2,1,0:T(1,128)S(1)}, u32[]{:S(2)}, u32[]{:S(2)}) %all-to-all-start.1) | async-done | bytes 655392 | tf_op jit(solution)/shard_map/all_to_all | solution.py:635
  87.2 0.7 copy-done.7
  87.9 8.1 %shard_map.158 = f32[64,128]{1,0:T(8,128)S(1)} custom-call(s32[4]{0:T(128)S(1)} %copy-done.7, s32[512]{0:T(512)} %counts_any.1, s32[512,128]{1,0:T(8,128)} %table_any.1, f32[4,192]{1,0:T(4,128)} %target_any.1, f32[128,1,1280]{2,1,0:T(1,128)S(1)} %all-to-all-done.1.source_ref, f32[32,128]{1,0:T(8,128)S(1)} %get-tuple-element.18.z1_ref), custom_call_target="tpu_custom_call" | custom-call | bytes 4194304 | tf_op jit(solution)/shard_map/pallas_call | solution.py:568
  96.0 6.1 %all_to_all.16.group_ref = f32[4,64,128]{2,1,0:T(8,128)S(1)} all-to-all(f32[4,64,128]{2,1,0:T(8,128)S(1)} %broadcast_in_dim.3), channel_id=1, replica_groups=mesh['leaf'=128,'sub'=4] {'sub'}, dimensions={0} | all-to-all | bytes 262144 | tf_op jit(solution)/shard_map/all_to_all | solution.py:698
  102.0 3.8 %shard_map.159 = f32[16,2048]{1,0:T(8,128)} custom-call(s32[4]{0:T(128)S(1)} %copy-done.7, s32[32]{0:T(128)} %leaf_any.3, s32[16]{0:T(128)} %cluster_any.5, f32[4,64,128]{2,1,0:T(8,128)S(1)} %all_to_all.16.group_ref, f32[16,2048]{1,0:T(8,128)S(1)} %get-tuple-element.16.near_any.near_ref, f32[16,2048]{1,0:T(8,128)S(1)} %get-tuple-element.19.far_ref, ...), custom_call_target="tpu_custom_call" | custom-call | bytes 4194304 | tf_op jit(solution)/shard_map/pallas_call | solution.py:568
  (28 shorter events, 0.2 us)
Async XLA Ops:
  0.0 1.2 %copy-start.11 = (f32[32,4096]{1,0:T(8,128)S(1)}, f32[32,4096]{1,0:T(8,128)}, u32[]{:S(2)}) copy-start(f32[32,4096]{1,0:T(8,128)} %param.19) | copy-start | bytes 1572868
  1.2 1.0 copy-start.12
  2.8 53.7 %copy-start.5 = (s32[4]{0:T(128)}, s32[4]{0:T(128)S(1)}, u32[]{:S(2)}) copy-start(s32[4]{0:T(128)S(1)} %pad_add_fusion.base) | copy-start | bytes 52
  5.9 22.5 %copy-start.10 = (f32[40,2048]{1,0:T(8,128)}, f32[40,2048]{1,0:T(8,128)S(1)}, u32[]{:S(2)}) copy-start(f32[40,2048]{1,0:T(8,128)S(1)} %get-tuple-element.13.own_any) | copy-start | bytes 983044
  5.9 22.5 %collective-permute-start.1 = (f32[40,2048]{1,0:T(8,128)S(1)}, f32[40,2048]{1,0:T(8,128)S(1)}, u32[]{:S(2)}, u32[]{:S(2)}) collective-permute-start(f32[40,2048]{1,0:T(8,128)S(1)} %get-tuple-element.13.own_any), channel_id=1, source_target_pairs={{1,0},{2,1},{3,2},{4,3},{5,4},{6,5},{7,6},{8,7},{9,8},{10,9},{11,1... | collective-permute-start | bytes 983048 | tf_op jit(solution)/shard_map/ppermute | solution.py:582
  8.0 20.4 %collective-permute-start = (f32[40,2048]{1,0:T(8,128)S(1)}, f32[40,2048]{1,0:T(8,128)S(1)}, u32[]{:S(2)}, u32[]{:S(2)}) collective-permute-start(f32[40,2048]{1,0:T(8,128)S(1)} %get-tuple-element.13.own_any), channel_id=1, source_target_pairs={{0,1},{1,2},{2,3},{3,4},{4,5},{5,6},{6,7},{7,8},{8,9},{9,10},{10,1... | collective-permute-start | bytes 983048 | tf_op jit(solution)/shard_map/ppermute | solution.py:582
  10.3 18.2 %copy-start.3 = (f32[16,192]{1,0:T(8,128)S(1)}, f32[16,192]{1,0:T(8,128)}, u32[]{:S(2)}) copy-start(f32[16,192]{1,0:T(8,128)} %cluster_skel_ref.1) | copy-start | bytes 36868
  10.3 18.2 %copy-start.4 = (f32[4,192]{1,0:T(4,128)S(1)}, f32[4,192]{1,0:T(4,128)}, u32[]{:S(2)}) copy-start(f32[4,192]{1,0:T(4,128)} %target_any.1) | copy-start | bytes 9220
  28.4 1.3 %copy-start.1 = (f32[40,2048]{1,0:T(8,128)}, f32[40,2048]{1,0:T(8,128)S(1)}, u32[]{:S(2)}) copy-start(f32[40,2048]{1,0:T(8,128)S(1)} %collective-permute-done.1.after_any) | copy-start | bytes 983044
  28.5 1.3 %copy-start.2 = (f32[40,2048]{1,0:T(8,128)}, f32[40,2048]{1,0:T(8,128)S(1)}, u32[]{:S(2)}) copy-start(f32[40,2048]{1,0:T(8,128)S(1)} %collective-permute-done.before_any) | copy-start | bytes 983044
  29.8 0.9 copy-start
  30.6 25.1 %copy-start.13 = (s32[32,24]{0,1:T(8,128)S(1)}, s32[32,24]{0,1:T(8,128)}, u32[]{:S(2)}) copy-start(s32[32,24]{0,1:T(8,128)} %param.21) | copy-start | bytes 9220
  30.6 56.6 %all-to-all-start.1 = ((f32[128,1,1280]{2,1,0:T(1,128)}), f32[128,1,1280]{2,1,0:T(1,128)S(1)}, u32[]{:S(2)}, u32[]{:S(2)}) async-start(f32[128,1,1280]{2,1,0:T(1,128)} %copy-done), calls=%async_computation.1 | async-start | bytes 1310720 | tf_op jit(solution)/shard_map/all_to_all | solution.py:635
  47.1 27.7 %collective-permute-start.3 = (f32[152,128]{1,0:T(8,128)}, f32[152,128]{1,0:T(8,128)}, u32[]{:S(2)}, u32[]{:S(2)}) collective-permute-start(f32[152,128]{1,0:T(8,128)} %get-tuple-element.17.own_ref), channel_id=1, source_target_pairs={{4,0},{8,4},{12,8},{16,12},{20,16},{24,20},{28,24},{32,28},{36,32}... | collective-permute-start | bytes 233480 | tf_op jit(solution)/shard_map/ppermute | solution.py:588
  53.8 27.0 %collective-permute-start.2 = (f32[152,128]{1,0:T(8,128)}, f32[152,128]{1,0:T(8,128)}, u32[]{:S(2)}, u32[]{:S(2)}) collective-permute-start(f32[152,128]{1,0:T(8,128)} %get-tuple-element.17.own_ref), channel_id=1, source_target_pairs={{0,4},{4,8},{8,12},{12,16},{16,20},{20,24},{24,28},{28,32},{32,36}... | collective-permute-start | bytes 233480 | tf_op jit(solution)/shard_map/ppermute | solution.py:588
  74.2 6.6 %copy-start.6 = (s32[4]{0:T(128)S(1)}, s32[4]{0:T(128)}, u32[]{:S(2)}) copy-start(s32[4]{0:T(128)} %copy-done.5) | copy-start | bytes 52
  84.0 0.6 copy-start.8
  87.2 0.7 copy-start.7
  95.9 6.1 %copy-start.9 = (s32[16,128]{1,0:T(8,128)S(1)}, s32[16,128]{1,0:T(8,128)}, u32[]{:S(2)}) copy-start(s32[16,128]{1,0:T(8,128)} %copy-done.8) | copy-start | bytes 24580

commit v3 on v2

--- a/solution.py
+++ b/solution.py
@@ -5,7 +5,7 @@
 from jax import lax
 from jax.experimental import pallas as pl
 from jax.experimental.pallas import tpu as pltpu
-from jax.sharding import PartitionSpec as P
+from jax.sharding import Mesh, PartitionSpec as P
 
 COLS = 16
 LEAF = 64
@@ -20,6 +20,10 @@
 LD = 32
 C1 = 16
 SUB = 4
+XL = 2
+T2 = C2 * XL
+LEAF_AXES = ("yh", "z", "xh", "xl")
+FAR_AXES = ("yh", "z", "xh")
 PTS = LD * LEAF
 TILE = 128
 ROWS = 40
@@ -184,6 +188,10 @@
     for pair in range(C1 // 2):
         for k, row in enumerate(skeleton_rows(cluster_skel_ref, pair)):
             cluster_ref[TILE + 8 * k + pair : TILE + 8 * k + pair + 1, :] = row
+    for pair in range(C2 // 2):
+        for k, row in enumerate(skeleton_rows(top_skel_ref, pair)):
+            cluster_ref[TILE + 24 + 2 * k + pair : TILE + 25 + 2 * k + pair, :] = row
+    cluster_ref[TILE + 30 : TILE + 32, :] = jnp.zeros((2, TILE), F32)
     which = lax.broadcasted_iota(jnp.int32, (C2, 3 * RANK), 0)
     skel = jnp.sum(jnp.where(which == base[3], top_skel_ref[...], 0.0), axis=0, keepdims=True)
     load = joined([total[j : j + 1] for j in range(8)] + [skel, jnp.zeros((1, RANK), F32)])
@@ -411,27 +419,27 @@
 
 
 def top_kernel(
-    base, counts_any, table_any, target_any, source_ref, z1_ref,
-    out_ref, rows, spread_ref, order, lists, top_counts, table, target_ref, sems,
+    base, counts_any, table_any, source_ref, z1_ref, own_ref, before_ref, after_ref,
+    out_ref, rows, spread_ref, order, lists, top_counts, table, sems,
 ):
-    aligned = pl.multiple_of(base[1] // 8 * 8, 8)
-    copies = fetched(
-        [counts_any, table_any.at[pl.ds(aligned, 8)], target_any], [top_counts, table, target_ref], sems
-    )
-    out_ref[C2 * 8 :, :] = z1_ref[...]
+    aligned = pl.multiple_of(base[1] // T2 * T2, T2)
+    copies = fetched([counts_any, table_any.at[pl.ds(aligned, T2)]], [top_counts, table], sems)
+    for half in range(XL):
+        out_ref[half, C2 * 8 :, :] = z1_ref[...]
     for copy in copies:
         copy.wait()
     lane = lax.broadcasted_iota(jnp.int32, (8, TILE), 1)
     left = lane < RANK
     items = 0
-    for top in range(C2):
+    mine = base[4] * SUB + base[3]
+    for top in range(T2):
 
         def note(slot, found, top=top):
-            cluster = table[base[1] - aligned + top, slot]
-            lists[top, found] = cluster // SUB
-            return found + jnp.where(cluster % SUB == base[3], 1, 0)
-
-        found = lax.fori_loop(0, top_counts[base[1] + top], note, 0)
+            cluster = table[top, slot]
+            lists[top, found] = cluster // T2
+            return found + jnp.where(cluster % T2 == mine, 1, 0)
+
+        found = lax.fori_loop(0, top_counts[aligned + top], note, 0)
         for k in range(GROUP):
             lists[top, found + k] = -1
         first_item = items
@@ -441,22 +449,27 @@
             return count + 1
 
         items = lax.fori_loop(0, (found + GROUP - 1) // GROUP, plan, items)
-        skel = jnp.concatenate(
-            [target_ref[top : top + 1, k * RANK : (k + 1) * RANK] for k in range(3)]
-            + [jnp.zeros((5, RANK), F32)],
-            axis=0,
-        )
-        columns = joined([skel, jnp.zeros((8, RANK), F32)]).T
-        for k, axis in enumerate(spread(columns[:LEAF])):
-            spread_ref[top, k] = axis
         rows[top] = jnp.zeros((32, TILE), F32)
+    for half in range(XL):
+        for pair in range(C2 // 2):
+            picked = []
+            for k in range(3):
+                at = TILE + 24 + 2 * k + pair
+                other = before_ref if half == 0 else after_ref
+                picked.append(
+                    jnp.where(base[4] == half, own_ref[at : at + 1, :], other[at : at + 1, :])
+                )
+            columns = jnp.concatenate(picked + [jnp.zeros((5, TILE), F32)], axis=0).T
+            for unit in range(2):
+                for k, axis in enumerate(spread(columns[unit * RANK : (unit + 1) * RANK])):
+                    spread_ref[half * C2 + 2 * pair + unit, k] = axis
     for k in range(GROUP):
-        lists[C2, k] = -1
-    order[items] = C2 * (2 * MAXF2)
+        lists[T2, k] = -1
+    order[items] = T2 * (2 * MAXF2)
 
     def product(item):
         top, start = item // (2 * MAXF2), item % (2 * MAXF2)
-        target = jnp.minimum(top, C2 - 1)
+        target = jnp.minimum(top, T2 - 1)
         axes = [spread_ref[target, k] for k in range(3)]
         tiles, places = [], []
         for k in range(GROUP):
@@ -504,11 +517,12 @@
         return carry
 
     lax.fori_loop(0, (items + 1) // 2, step, 0)
-    for top in range(C2):
+    for top in range(T2):
         total = rows[top]
         total = total[:COLS] + total[COLS:]
         total = (total + pltpu.roll(total, RANK, 1)) * INV_FOUR_PI
-        out_ref[top * 8 : top * 8 + 8, :] = jnp.where(left, total[:8], total[8:])
+        half, at = divmod(top, C2)
+        out_ref[half, at * 8 : at * 8 + 8, :] = jnp.where(left, total[:8], total[8:])
 
 
 def downward_kernel(
@@ -519,7 +533,7 @@
     copies = fetched([leaf_any, cluster_any], [leaf_parent, cluster_parent], sems)
     for top in range(C2):
         tile = group_ref[0, top * 8 : top * 8 + 8, :]
-        for part in range(1, SUB):
+        for part in range(1, XL * SUB):
             tile = tile + group_ref[part, top * 8 : top * 8 + 8, :]
         z2_acc[top] = from_tile(tile)
     for copy in copies:
@@ -533,7 +547,7 @@
             cluster = group * GROUP + k
             part, place = divmod(cluster, C1 // SUB)
             at = C2 * 8 + place * 8
-            local = from_tile(group_ref[part, at : at + 8, :])
+            local = from_tile(group_ref[base[4] * SUB + part, at : at + 8, :])
             w1_acc[cluster] = local + wide[k * COLS : (k + 1) * COLS, k * RANK : (k + 1) * RANK]
     locals_ = []
     for group in range(LD // GROUP):
@@ -577,15 +591,15 @@
 
 
 def linear_shift(value, step):
-    size = lax.axis_size("leaf") * lax.axis_size("sub")
+    size = lax.axis_size(LEAF_AXES) * lax.axis_size("sub")
     pairs = [(i, i + step) for i in range(size) if 0 <= i + step < size]
-    return lax.ppermute(value, ("leaf", "sub"), pairs)
+    return lax.ppermute(value, (*LEAF_AXES, "sub"), pairs)
 
 
 def leaf_shift(value, step):
-    size = lax.axis_size("leaf")
+    size = lax.axis_size(LEAF_AXES)
     pairs = [(i, i + step) for i in range(size) if 0 <= i + step < size]
-    return lax.ppermute(value, "leaf", pairs)
+    return lax.ppermute(value, LEAF_AXES, pairs)
 
 
 def local(
@@ -593,11 +607,13 @@
     leaf_parent, cluster_skeleton, far_cluster, cluster_transfer, cluster_parent, top_skeleton,
     far_top, top_counts,
 ):
-    leaf_count = lax.axis_size("leaf")
-    leaf_pos = lax.axis_index("leaf")
+    peers = lax.axis_size(FAR_AXES)
+    leaf_pos = lax.axis_index(LEAF_AXES)
     sub_pos = lax.axis_index("sub")
     first_leaf = (leaf_pos * SUB + sub_pos) * LD
-    base = jnp.stack([leaf_pos * C1, leaf_pos * C2, first_leaf, sub_pos]).astype(jnp.int32)
+    base = jnp.stack(
+        [leaf_pos * C1, leaf_pos * C2, first_leaf, sub_pos, lax.axis_index("xl")]
+    ).astype(jnp.int32)
     basis = leaf_basis.reshape(LD, LEAF, RANK)
     transfer = leaf_transfer.reshape(LD, RANK, RANK)
     cluster_trans = cluster_transfer.reshape(C1, RANK, RANK)
@@ -628,11 +644,11 @@
         [base],
         [],
         [received, cluster_skeleton, top_skeleton],
-        [((C1 * 8 + 24, TILE), F32), ((leaf_count, 1, 10 * TILE), F32)],
+        [((C1 * 8 + 32, TILE), F32), ((peers, 1, 10 * TILE), F32)],
         [],
         loose=[before, after],
     )
-    top_all = lax.all_to_all(top_send, "leaf", 0, 0, tiled=True)
+    top_all = lax.all_to_all(top_send, FAR_AXES, 0, 0, tiled=True)
     cl_before = leaf_shift(cl_own, 1)
     cl_after = leaf_shift(cl_own, -1)
 
@@ -681,23 +697,22 @@
     (share,) = call(
         top_kernel,
         [base],
-        [top_counts, far_top, top_skeleton],
-        [top_all, z1],
-        [(((C2 + C1 // SUB) * 8, TILE), F32)],
+        [top_counts, far_top],
+        [top_all, z1, cl_own, cl_before, cl_after],
+        [((XL, (C2 + C1 // SUB) * 8, TILE), F32)],
         [
-            pltpu.VMEM((C2, 32, TILE), F32),
-            pltpu.VMEM((C2, 3, LEAF, TILE), F32),
-            pltpu.SMEM((C2 * MAXF2 // GROUP + 8,), jnp.int32),
-            pltpu.SMEM((C2 + 1, 2 * MAXF2), jnp.int32),
+            pltpu.VMEM((T2, 32, TILE), F32),
+            pltpu.VMEM((T2, 3, LEAF, TILE), F32),
+            pltpu.SMEM((T2 * MAXF2 // GROUP + 8,), jnp.int32),
+            pltpu.SMEM((T2 + 1, 2 * MAXF2), jnp.int32),
             pltpu.SMEM(top_counts.shape, jnp.int32),
-            pltpu.SMEM((8, MAXF2), jnp.int32),
-            pltpu.VMEM((C2, 3 * RANK), F32),
-            pltpu.SemaphoreType.DMA((3,)),
+            pltpu.SMEM((T2, MAXF2), jnp.int32),
+            pltpu.SemaphoreType.DMA((2,)),
         ],
     )
-    group = lax.all_to_all(
-        jnp.broadcast_to(share, (SUB, (C2 + C1 // SUB) * 8, TILE)), "sub", 0, 0
-    )
+    rows = (C2 + C1 // SUB) * 8
+    spreading = jnp.broadcast_to(share[:, None], (XL, SUB, rows, TILE)).reshape(XL * SUB, rows, TILE)
+    group = lax.all_to_all(spreading, ("xl", "sub"), 0, 0, tiled=True)
     (product,) = call(
         downward_kernel,
         [base],
@@ -717,12 +732,13 @@
 
 
 def solution(mesh):
-    both = ("leaf", "sub")
+    fine = Mesh(mesh.devices.reshape(2, 16, 4 // XL, XL, SUB), (*LEAF_AXES, "sub"))
+    both = (*LEAF_AXES, "sub")
     placed = (
         P(None, both), P(both, None), P(None, both), P(both, None), P(both, None), P(both, None),
-        P(both, None), P(both, None), P(both), P("leaf", None), P("leaf", None), P("leaf", None),
-        P("leaf"), P("leaf", None), P(), P(),
+        P(both, None), P(both, None), P(both), P(LEAF_AXES, None), P(LEAF_AXES, None),
+        P(LEAF_AXES, None), P(LEAF_AXES), P(LEAF_AXES, None), P(), P(),
     )
     return jax.shard_map(
-        local, mesh=mesh, in_specs=placed, out_specs=P(None, both), check_vma=False
-    )
+        local, mesh=fine, in_specs=placed, out_specs=P(None, both), check_vma=False
+    )

time: 107 us -> 96.3 us (0.900)
  waiting for transfers between devices: 9.19 us -> 0.01 us
  blocking collectives: 24.2 us -> 26.8 us
  local copies, waits for them, and re-layouts: 5.49 us -> 3.46 us
  Pallas kernels: 37.2 us -> 35.4 us
    ppermute x4, waiting for transfers between devices: 6.61 us -> 0.01 us  [the longest x2 0.01 us: leaf_shift(): return lax.ppermute(value, LEAF_AXES, pairs)]
    all_to_all x1, waiting for transfers between devices: 2.59 us -> 0.01 us  [local(): top_all = lax.all_to_all(top_send, FAR_AXES, 0, 0, tiled=True)]
    all_to_all x1, blocking collectives: 6.06 us -> 8.62 us  [local(): group = lax.all_to_all(spreading, ('xl', 'sub'), 0, 0, tiled=True)]
    unnamed x29 -> x17, local copies, waits for them, and re-layouts: 3.46 us -> 1.33 us
    all_to_all x1, starting transfers between devices: 16.5 us -> 14.4 us  [local(): top_all = lax.all_to_all(top_send, FAR_AXES, 0, 0, tiled=True)]
    pallas_call x6, Pallas kernels: 37.2 us -> 35.4 us  [call(): pl.pallas_call(body, in_specs=[SMEM] * len(scalars) + [ANY] * (len(loose)...]
    ppermute x4, starting transfers between devices: 12.9 us -> 14.2 us  [the longest x2 9.82 us: leaf_shift(): return lax.ppermute(value, LEAF_AXES, pairs)]
  transfers between devices with their start and end apart: 5 -> 5, of which waited for: 3 -> 0; matrix products, arithmetic and copies ran while one was open for 1% -> 1% of each run, Pallas kernels for 20% -> 22%
where the time goes in v3:
time: 96.3 us; the launch traced here: 94.4 us
  Pallas kernels  35.4 us (37%)
  starting transfers between devices  28.6 us (30%)
  blocking collectives  26.8 us (28%)
  local copies, waits for them, and re-layouts  3.46 us (4%)
    pallas_call x6, Pallas kernels, call(): pl.pallas_call(body, in_specs=[SMEM] * len(scalars) + [ANY] * (len(loose)...  35.4 us
    all_to_all x1, blocking collectives, local(): received = lax.all_to_all(send, 'sub', 0, 0)  18.2 us
    all_to_all x1, starting transfers between devices, local(): top_all = lax.all_to_all(top_send, FAR_AXES, 0, 0, tiled=True)  14.4 us
    ppermute x2, starting transfers between devices, leaf_shift(): return lax.ppermute(value, LEAF_AXES, pairs)  9.82 us
    all_to_all x1, blocking collectives, local(): group = lax.all_to_all(spreading, ('xl', 'sub'), 0, 0, tiled=True)  8.62 us
    ppermute x2, starting transfers between devices, linear_shift(): return lax.ppermute(value, (*LEAF_AXES, 'sub'), pairs)  4.33 us
  transfers between devices with their start and end apart: 5, of which 0 were waited for; matrix products, arithmetic and copies ran while one was open for 1% of the time, Pallas kernels for 22%

profile of v3, /device:TPU:24, one launch (start us, length us, event | category | flops | bytes accessed | tf_op | source)
XLA Modules:
  0.0 94.4 jit_solution(7795715645579244033)
XLA Ops:
  0.0 1.2 %reshape.15.cluster_transfer_ref = f32[16,64,64]{2,1,0:T(8,128)S(1)} reshape(f32[16,4096]{1,0:T(8,128)} %param.27) | data formatting | bytes 524288 | tf_op jit(solution)/shard_map/reshape | solution.py:619
  1.2 0.0 copy-start.6
  1.2 0.4 reshape.13.basis_ref
  1.7 0.6 copy-done.6
  2.3 0.4 reshape.14.transfer_ref
  2.7 0.1 stack.23.base
  2.8 3.1 %shard_map.154 = (f32[40,2048]{1,0:T(8,128)S(1)}, f32[4,136,128]{2,1,0:T(8,128)S(1)}) custom-call(s32[5]{0:T(128)S(1)} %stack.23.base, f32[16,2048]{1,0:T(8,128)} %x_any.1, s32[1,2048]{1,0:T(1,128)} %order_any.3, f32[3,2048]{1,0:T(4,128)} %points_any.1, f32[32,192]{1,0:T(8,128)} %skel_any.1, s32[32]{0:T(128)} %leaf_any.3, s32[16]{0:T(128)} %cluster_any.5, ...), custom_call_target="tpu_custom_call" | custom-call | bytes 4194304 | tf_op jit(solution)/shard_map/pallas_call | solution.py:582
  5.9 2.1 %collective-permute-start.1 = (f32[40,2048]{1,0:T(8,128)S(1)}, f32[40,2048]{1,0:T(8,128)S(1)}, u32[]{:S(2)}, u32[]{:S(2)}) collective-permute-start(f32[40,2048]{1,0:T(8,128)S(1)} %get-tuple-element.13.own_any), channel_id=1, source_target_pairs={{1,0},{2,1},{3,2},{4,3},{5,4},{6,5},{7,6},{8,7},{9,8},{10,9},{11,1... | collective-permute-start | bytes 983048 | tf_op jit(solution)/shard_map/ppermute | solution.py:596
  8.0 2.2 %collective-permute-start = (f32[40,2048]{1,0:T(8,128)S(1)}, f32[40,2048]{1,0:T(8,128)S(1)}, u32[]{:S(2)}, u32[]{:S(2)}) collective-permute-start(f32[40,2048]{1,0:T(8,128)S(1)} %get-tuple-element.13.own_any), channel_id=1, source_target_pairs={{0,1},{1,2},{2,3},{3,4},{4,5},{5,6},{6,7},{7,8},{8,9},{9,10},{10,1... | collective-permute-start | bytes 983048 | tf_op jit(solution)/shard_map/ppermute | solution.py:596
  10.3 0.0 copy-start.2
  10.3 0.0 copy-start.3
  10.3 18.2 %all_to_all.15.received_ref = f32[4,136,128]{2,1,0:T(8,128)S(1)} all-to-all(f32[4,136,128]{2,1,0:T(8,128)S(1)} %get-tuple-element.14), channel_id=1, replica_groups=mesh['yh'=2,'z'=16,'xh'=2,'xl'=2,'sub'=4] {'sub'}, dimensions={0} | all-to-all | bytes 557056 | tf_op jit(solution)/shard_map/all_to_all | solution.py:641
  28.4 0.0 collective-permute-done.1.after_any
  28.5 1.3 %shard_map.155 = (f32[160,128]{1,0:T(8,128)S(1)}, f32[64,1,1280]{2,1,0:T(1,128)}) custom-call(s32[5]{0:T(128)S(1)} %stack.23.base, f32[40,2048]{1,0:T(8,128)S(1)} %collective-permute-done.before_any, f32[40,2048]{1,0:T(8,128)S(1)} %collective-permute-done.1.after_any, f32[4,136,128]{2,1,0:T(8,128)S(1)} %all_to_all.15.received_ref, f32[16,192]{1,0:T(8,128)S(1)} %copy-done.2, ...), custom_call_target="tpu_custom_call" | custom-call | bytes 4194304 | tf_op jit(solution)/shard_map/pallas_call | solution.py:582
  29.8 0.0 copy-start.7
  29.8 14.4 %all-to-all-start.1 = ((f32[64,1,1280]{2,1,0:T(1,128)}), f32[64,1,1280]{2,1,0:T(1,128)S(1)}, u32[]{:S(2)}, u32[]{:S(2)}) async-start(f32[64,1,1280]{2,1,0:T(1,128)} %get-tuple-element.15), calls=%async_computation.1 | async-start | bytes 655360 | tf_op jit(solution)/shard_map/all_to_all | solution.py:651
  44.2 7.9 %collective-permute-start.3 = (f32[160,128]{1,0:T(8,128)S(1)}, f32[160,128]{1,0:T(8,128)S(1)}, u32[]{:S(2)}, u32[]{:S(2)}) collective-permute-start(f32[160,128]{1,0:T(8,128)S(1)} %get-tuple-element.17.own_ref), channel_id=1, source_target_pairs={{4,0},{8,4},{12,8},{16,12},{20,16},{24,20},{28,24},{32,28},{36,32}... | collective-permute-start | bytes 245768 | tf_op jit(solution)/shard_map/ppermute | solution.py:602
  52.1 1.9 %collective-permute-start.2 = (f32[160,128]{1,0:T(8,128)S(1)}, f32[160,128]{1,0:T(8,128)S(1)}, u32[]{:S(2)}, u32[]{:S(2)}) collective-permute-start(f32[160,128]{1,0:T(8,128)S(1)} %get-tuple-element.17.own_ref), channel_id=1, source_target_pairs={{0,4},{4,8},{8,12},{12,16},{16,20},{20,24},{24,28},{28,32},{32,36}... | collective-permute-start | bytes 245768 | tf_op jit(solution)/shard_map/ppermute | solution.py:602
  54.1 0.7 copy.17.far_any
  54.8 17.7 %shard_map.156 = (f32[16,2048]{1,0:T(8,128)S(1)}, f32[16,2048]{1,0:T(8,128)S(1)}) custom-call(s32[5]{0:T(128)S(1)} %stack.23.base, f32[40,2048]{1,0:T(8,128)} %copy-done.4, f32[40,2048]{1,0:T(8,128)} %copy-done.1, f32[40,2048]{1,0:T(8,128)} %copy-done, s32[32,27]{1,0:T(8,128)} %near_any.1, s32[32,24]{1,0:T(8,128)} %copy.17.far_any), custom_call_target="tpu_custom_call" | custom-call | flops 140000000 | bytes 4194304 | tf_op jit(solution)/shard_map/pallas_call | solution.py:582
  72.5 3.2 %shard_map.157 = (f32[32,128]{1,0:T(8,128)S(1)}, s32[16,128]{1,0:T(8,128)S(1)}) custom-call(s32[5]{0:T(128)S(1)} %stack.23.base, f32[16,2048]{1,0:T(8,128)S(1)} %get-tuple-element.16.near_any.near_ref, s32[16,16]{1,0:T(8,128)} %cluster_any.4, s32[1,2048]{1,0:T(1,128)} %order_any.3, f32[160,128]{1,0:T(8,128)S(1)} %get-tuple-element.17.own_ref, ...), custom_call_target="tpu_custom_call" | custom-call | flops 5242880 | bytes 4194304 | tf_op jit(solution)/shard_map/pallas_call | solution.py:582
  75.7 6.3 %shard_map.158 = f32[2,64,128]{2,1,0:T(8,128)S(1)} custom-call(s32[5]{0:T(128)S(1)} %stack.23.base, s32[512]{0:T(512)} %counts_any.1, s32[512,128]{1,0:T(8,128)} %table_any.1, f32[64,1,1280]{2,1,0:T(1,128)S(1)} %all-to-all-done.1.source_ref, f32[32,128]{1,0:T(8,128)S(1)} %get-tuple-element.18.z1_ref, f32[160,128]{1,0:T(8,128)S(1)} %get-tuple-element.17.own_ref, ...), custom_call_target="tpu_custom_call" | custom-call | bytes 4194304 | tf_op jit(solution)/shard_map/pallas_call | solution.py:582
  82.0 8.6 %all_to_all.16.group_ref = f32[8,64,128]{2,1,0:T(8,128)S(1)} all-to-all(f32[8,64,128]{2,1,0:T(8,128)S(1)} %bitcast.6), channel_id=1, replica_groups=mesh['yh'=2,'z'=16,'xh'=2,'xl'=2,'sub'=4] {'xl','sub'}, dimensions={0} | all-to-all | bytes 524288 | tf_op jit(solution)/shard_map/all_to_all | solution.py:715
  90.7 3.8 %shard_map.159 = f32[16,2048]{1,0:T(8,128)} custom-call(s32[5]{0:T(128)S(1)} %stack.23.base, s32[32]{0:T(128)} %leaf_any.3, s32[16]{0:T(128)} %cluster_any.5, f32[8,64,128]{2,1,0:T(8,128)S(1)} %all_to_all.16.group_ref, f32[16,2048]{1,0:T(8,128)S(1)} %get-tuple-element.16.near_any.near_ref, f32[16,2048]{1,0:T(8,128)S(1)} %get-tuple-element.19.far_ref, ...), custom_call_target="tpu_custom_call" | custom-call | bytes 4194304 | tf_op jit(solution)/shard_map/pallas_call | solution.py:582
  (16 shorter events, 0.1 us)
Async XLA Ops:
  0.0 1.2 %copy-start.5 = (f32[32,4096]{1,0:T(8,128)S(1)}, f32[32,4096]{1,0:T(8,128)}, u32[]{:S(2)}) copy-start(f32[32,4096]{1,0:T(8,128)} %param.19) | copy-start | bytes 1572868
  1.2 1.0 %copy-start.6 = (f32[32,4096]{1,0:T(8,128)S(1)}, f32[32,4096]{1,0:T(8,128)}, u32[]{:S(2)}) copy-start(f32[32,4096]{1,0:T(8,128)} %param.23) | copy-start | bytes 1572868
  5.9 23.9 %copy-start.4 = (f32[40,2048]{1,0:T(8,128)}, f32[40,2048]{1,0:T(8,128)S(1)}, u32[]{:S(2)}) copy-start(f32[40,2048]{1,0:T(8,128)S(1)} %get-tuple-element.13.own_any) | copy-start | bytes 983044
  5.9 22.5 %collective-permute-start.1 = (f32[40,2048]{1,0:T(8,128)S(1)}, f32[40,2048]{1,0:T(8,128)S(1)}, u32[]{:S(2)}, u32[]{:S(2)}) collective-permute-start(f32[40,2048]{1,0:T(8,128)S(1)} %get-tuple-element.13.own_any), channel_id=1, source_target_pairs={{1,0},{2,1},{3,2},{4,3},{5,4},{6,5},{7,6},{8,7},{9,8},{10,9},{11,1... | collective-permute-start | bytes 983048 | tf_op jit(solution)/shard_map/ppermute | solution.py:596
  8.0 20.4 %collective-permute-start = (f32[40,2048]{1,0:T(8,128)S(1)}, f32[40,2048]{1,0:T(8,128)S(1)}, u32[]{:S(2)}, u32[]{:S(2)}) collective-permute-start(f32[40,2048]{1,0:T(8,128)S(1)} %get-tuple-element.13.own_any), channel_id=1, source_target_pairs={{0,1},{1,2},{2,3},{3,4},{4,5},{5,6},{6,7},{7,8},{8,9},{9,10},{10,1... | collective-permute-start | bytes 983048 | tf_op jit(solution)/shard_map/ppermute | solution.py:596
  10.3 18.2 %copy-start.2 = (f32[16,192]{1,0:T(8,128)S(1)}, f32[16,192]{1,0:T(8,128)}, u32[]{:S(2)}) copy-start(f32[16,192]{1,0:T(8,128)} %cluster_skel_ref.1) | copy-start | bytes 36868
  10.3 18.2 %copy-start.3 = (f32[4,192]{1,0:T(4,128)S(1)}, f32[4,192]{1,0:T(4,128)}, u32[]{:S(2)}) copy-start(f32[4,192]{1,0:T(4,128)} %top_skel_ref.1) | copy-start | bytes 9220
  28.4 1.4 %copy-start = (f32[40,2048]{1,0:T(8,128)}, f32[40,2048]{1,0:T(8,128)S(1)}, u32[]{:S(2)}) copy-start(f32[40,2048]{1,0:T(8,128)S(1)} %collective-permute-done.1.after_any) | copy-start | bytes 983044
  28.5 1.3 %copy-start.1 = (f32[40,2048]{1,0:T(8,128)}, f32[40,2048]{1,0:T(8,128)S(1)}, u32[]{:S(2)}) copy-start(f32[40,2048]{1,0:T(8,128)S(1)} %collective-permute-done.before_any) | copy-start | bytes 983044
  29.8 24.3 %copy-start.7 = (s32[32,24]{0,1:T(8,128)S(1)}, s32[32,24]{0,1:T(8,128)}, u32[]{:S(2)}) copy-start(s32[32,24]{0,1:T(8,128)} %param.21) | copy-start | bytes 9220
  29.8 45.9 %all-to-all-start.1 = ((f32[64,1,1280]{2,1,0:T(1,128)}), f32[64,1,1280]{2,1,0:T(1,128)S(1)}, u32[]{:S(2)}, u32[]{:S(2)}) async-start(f32[64,1,1280]{2,1,0:T(1,128)} %get-tuple-element.15), calls=%async_computation.1 | async-start | bytes 655360 | tf_op jit(solution)/shard_map/all_to_all | solution.py:651
  44.2 28.3 %collective-permute-start.3 = (f32[160,128]{1,0:T(8,128)S(1)}, f32[160,128]{1,0:T(8,128)S(1)}, u32[]{:S(2)}, u32[]{:S(2)}) collective-permute-start(f32[160,128]{1,0:T(8,128)S(1)} %get-tuple-element.17.own_ref), channel_id=1, source_target_pairs={{4,0},{8,4},{12,8},{16,12},{20,16},{24,20},{28,24},{32,28},{36,32}... | collective-permute-start | bytes 245768 | tf_op jit(solution)/shard_map/ppermute | solution.py:602
  52.1 20.4 %collective-permute-start.2 = (f32[160,128]{1,0:T(8,128)S(1)}, f32[160,128]{1,0:T(8,128)S(1)}, u32[]{:S(2)}, u32[]{:S(2)}) collective-permute-start(f32[160,128]{1,0:T(8,128)S(1)} %get-tuple-element.17.own_ref), channel_id=1, source_target_pairs={{0,4},{4,8},{8,12},{12,16},{16,20},{20,24},{24,28},{28,32},{32,36}... | collective-permute-start | bytes 245768 | tf_op jit(solution)/shard_map/ppermute | solution.py:602

commit v4 on v3

--- a/solution.py
+++ b/solution.py
@@ -347,7 +347,7 @@
                     rows_ref[2 * pair + unit] = part[:COLS] + part[COLS:]
             return carry
 
-        lax.fori_loop(0, LD // 2, leaf_step, 0, unroll=4)
+        lax.fori_loop(0, LD // 2, leaf_step, 0, unroll=8)
 
     pl.run_scoped(
         lambda first, second: leaf_pair((first, second)),
@@ -424,32 +424,8 @@
 ):
     aligned = pl.multiple_of(base[1] // T2 * T2, T2)
     copies = fetched([counts_any, table_any.at[pl.ds(aligned, T2)]], [top_counts, table], sems)
-    for half in range(XL):
-        out_ref[half, C2 * 8 :, :] = z1_ref[...]
-    for copy in copies:
-        copy.wait()
-    lane = lax.broadcasted_iota(jnp.int32, (8, TILE), 1)
-    left = lane < RANK
-    items = 0
-    mine = base[4] * SUB + base[3]
-    for top in range(T2):
-
-        def note(slot, found, top=top):
-            cluster = table[top, slot]
-            lists[top, found] = cluster // T2
-            return found + jnp.where(cluster % T2 == mine, 1, 0)
-
-        found = lax.fori_loop(0, top_counts[aligned + top], note, 0)
-        for k in range(GROUP):
-            lists[top, found + k] = -1
-        first_item = items
-
-        def plan(quad, count, top=top, first_item=first_item):
-            order[first_item + quad] = top * (2 * MAXF2) + GROUP * quad
-            return count + 1
-
-        items = lax.fori_loop(0, (found + GROUP - 1) // GROUP, plan, items)
-        rows[top] = jnp.zeros((32, TILE), F32)
+    for peer in range(XL * SUB):
+        out_ref[peer, C2 * 8 :, :] = z1_ref[...]
     for half in range(XL):
         for pair in range(C2 // 2):
             picked = []
@@ -463,6 +439,30 @@
             for unit in range(2):
                 for k, axis in enumerate(spread(columns[unit * RANK : (unit + 1) * RANK])):
                     spread_ref[half * C2 + 2 * pair + unit, k] = axis
+    for copy in copies:
+        copy.wait()
+    lane = lax.broadcasted_iota(jnp.int32, (8, TILE), 1)
+    left = lane < RANK
+    items = 0
+    mine = base[4] * SUB + base[3]
+    for top in range(T2):
+
+        def note(slot, found, top=top):
+            cluster = table[top, slot]
+            lists[top, found] = cluster // T2
+            return found + jnp.where(cluster % T2 == mine, 1, 0)
+
+        found = lax.fori_loop(0, top_counts[aligned + top], note, 0)
+        for k in range(GROUP):
+            lists[top, found + k] = -1
+        first_item = items
+
+        def plan(quad, count, top=top, first_item=first_item):
+            order[first_item + quad] = top * (2 * MAXF2) + GROUP * quad
+            return count + 1
+
+        items = lax.fori_loop(0, (found + GROUP - 1) // GROUP, plan, items)
+        rows[top] = jnp.zeros((32, TILE), F32)
     for k in range(GROUP):
         lists[T2, k] = -1
     order[items] = T2 * (2 * MAXF2)
@@ -522,7 +522,9 @@
         total = total[:COLS] + total[COLS:]
         total = (total + pltpu.roll(total, RANK, 1)) * INV_FOUR_PI
         half, at = divmod(top, C2)
-        out_ref[half, at * 8 : at * 8 + 8, :] = jnp.where(left, total[:8], total[8:])
+        tile = jnp.where(left, total[:8], total[8:])
+        for peer in range(half * SUB, half * SUB + SUB):
+            out_ref[peer, at * 8 : at * 8 + 8, :] = tile
 
 
 def downward_kernel(
@@ -699,7 +701,7 @@
         [base],
         [top_counts, far_top],
         [top_all, z1, cl_own, cl_before, cl_after],
-        [((XL, (C2 + C1 // SUB) * 8, TILE), F32)],
+        [((XL * SUB, (C2 + C1 // SUB) * 8, TILE), F32)],
         [
             pltpu.VMEM((T2, 32, TILE), F32),
             pltpu.VMEM((T2, 3, LEAF, TILE), F32),
@@ -710,9 +712,7 @@
             pltpu.SemaphoreType.DMA((2,)),
         ],
     )
-    rows = (C2 + C1 // SUB) * 8
-    spreading = jnp.broadcast_to(share[:, None], (XL, SUB, rows, TILE)).reshape(XL * SUB, rows, TILE)
-    group = lax.all_to_all(spreading, ("xl", "sub"), 0, 0, tiled=True)
+    group = lax.all_to_all(share, ("xl", "sub"), 0, 0, tiled=True)
     (product,) = call(
         downward_kernel,
         [base],

time: 96.3 us -> 96.4 us (level); the launches traced: 94.4 us -> 96.8 us
  Pallas kernels: 35.4 us -> 37.5 us
    pallas_call x6, Pallas kernels: 35.4 us -> 37.5 us  [call(): pl.pallas_call(body, in_specs=[SMEM] * len(scalars) + [ANY] * (len(loose)...]
  transfers between devices with their start and end apart: 5 -> 5, of which waited for: 0 -> 0; matrix products, arithmetic and copies ran while one was open for 1% -> 1% of each run, Pallas kernels for 22% -> 21%
where the time goes in v4:
time: 96.4 us; the launch traced here: 96.8 us
  Pallas kernels  37.5 us (39%)
  starting transfers between devices  28.7 us (30%)
  blocking collectives  26.8 us (28%)
  local copies, waits for them, and re-layouts  3.44 us (4%)
    pallas_call x6, Pallas kernels, call(): pl.pallas_call(body, in_specs=[SMEM] * len(scalars) + [ANY] * (len(loose)...  37.5 us
    all_to_all x1, blocking collectives, local(): received = lax.all_to_all(send, 'sub', 0, 0)  18.2 us
    all_to_all x1, starting transfers between devices, local(): top_all = lax.all_to_all(top_send, FAR_AXES, 0, 0, tiled=True)  14.4 us
    ppermute x2, starting transfers between devices, leaf_shift(): return lax.ppermute(value, LEAF_AXES, pairs)  10 us
    all_to_all x1, blocking collectives, local(): group = lax.all_to_all(share, ('xl', 'sub'), 0, 0, tiled=True)  8.62 us
    ppermute x2, starting transfers between devices, linear_shift(): return lax.ppermute(value, (*LEAF_AXES, 'sub'), pairs)  4.33 us
  transfers between devices with their start and end apart: 5, of which 0 were waited for; matrix products, arithmetic and copies ran while one was open for 1% of the time, Pallas kernels for 21%

profile of v4, /device:TPU:24, one launch (start us, length us, event | category | flops | bytes accessed | tf_op | source)
XLA Modules:
  0.0 96.8 jit_solution(12075554107635216830)
XLA Ops:
  0.0 1.2 %reshape.11.cluster_transfer_ref = f32[16,64,64]{2,1,0:T(8,128)S(1)} reshape(f32[16,4096]{1,0:T(8,128)} %param.27) | data formatting | bytes 524288 | tf_op jit(solution)/shard_map/reshape | solution.py:621
  1.2 0.0 copy-start.6
  1.2 0.4 reshape.9.basis_ref
  1.7 0.6 copy-done.6
  2.3 0.4 reshape.10.transfer_ref
  2.7 0.1 stack.23.base
  2.8 3.1 %shard_map.154 = (f32[40,2048]{1,0:T(8,128)S(1)}, f32[4,136,128]{2,1,0:T(8,128)S(1)}) custom-call(s32[5]{0:T(128)S(1)} %stack.23.base, f32[16,2048]{1,0:T(8,128)} %x_any.1, s32[1,2048]{1,0:T(1,128)} %order_any.3, f32[3,2048]{1,0:T(4,128)} %points_any.1, f32[32,192]{1,0:T(8,128)} %skel_any.1, s32[32]{0:T(128)} %leaf_any.3, s32[16]{0:T(128)} %cluster_any.5, ...), custom_call_target="tpu_custom_call" | custom-call | bytes 4194304 | tf_op jit(solution)/shard_map/pallas_call | solution.py:584
  5.9 2.1 %collective-permute-start.1 = (f32[40,2048]{1,0:T(8,128)S(1)}, f32[40,2048]{1,0:T(8,128)S(1)}, u32[]{:S(2)}, u32[]{:S(2)}) collective-permute-start(f32[40,2048]{1,0:T(8,128)S(1)} %get-tuple-element.13.own_any), channel_id=1, source_target_pairs={{1,0},{2,1},{3,2},{4,3},{5,4},{6,5},{7,6},{8,7},{9,8},{10,9},{11,1... | collective-permute-start | bytes 983048 | tf_op jit(solution)/shard_map/ppermute | solution.py:598
  8.0 2.2 %collective-permute-start = (f32[40,2048]{1,0:T(8,128)S(1)}, f32[40,2048]{1,0:T(8,128)S(1)}, u32[]{:S(2)}, u32[]{:S(2)}) collective-permute-start(f32[40,2048]{1,0:T(8,128)S(1)} %get-tuple-element.13.own_any), channel_id=1, source_target_pairs={{0,1},{1,2},{2,3},{3,4},{4,5},{5,6},{6,7},{7,8},{8,9},{9,10},{10,1... | collective-permute-start | bytes 983048 | tf_op jit(solution)/shard_map/ppermute | solution.py:598
  10.3 0.0 copy-start.2
  10.3 0.0 copy-start.3
  10.3 18.2 %all_to_all.15.received_ref = f32[4,136,128]{2,1,0:T(8,128)S(1)} all-to-all(f32[4,136,128]{2,1,0:T(8,128)S(1)} %get-tuple-element.14), channel_id=1, replica_groups=mesh['yh'=2,'z'=16,'xh'=2,'xl'=2,'sub'=4] {'sub'}, dimensions={0} | all-to-all | bytes 557056 | tf_op jit(solution)/shard_map/all_to_all | solution.py:643
  28.4 0.0 collective-permute-done.1.after_any
  28.5 1.3 %shard_map.155 = (f32[160,128]{1,0:T(8,128)S(1)}, f32[64,1,1280]{2,1,0:T(1,128)}) custom-call(s32[5]{0:T(128)S(1)} %stack.23.base, f32[40,2048]{1,0:T(8,128)S(1)} %collective-permute-done.before_any, f32[40,2048]{1,0:T(8,128)S(1)} %collective-permute-done.1.after_any, f32[4,136,128]{2,1,0:T(8,128)S(1)} %all_to_all.15.received_ref, f32[16,192]{1,0:T(8,128)S(1)} %copy-done.2, ...), custom_call_target="tpu_custom_call" | custom-call | bytes 4194304 | tf_op jit(solution)/shard_map/pallas_call | solution.py:584
  29.8 0.0 copy-start.7
  29.8 14.4 %all-to-all-start.1 = ((f32[64,1,1280]{2,1,0:T(1,128)}), f32[64,1,1280]{2,1,0:T(1,128)S(1)}, u32[]{:S(2)}, u32[]{:S(2)}) async-start(f32[64,1,1280]{2,1,0:T(1,128)} %get-tuple-element.15), calls=%async_computation.1 | async-start | bytes 655360 | tf_op jit(solution)/shard_map/all_to_all | solution.py:653
  44.2 7.9 %collective-permute-start.3 = (f32[160,128]{1,0:T(8,128)S(1)}, f32[160,128]{1,0:T(8,128)S(1)}, u32[]{:S(2)}, u32[]{:S(2)}) collective-permute-start(f32[160,128]{1,0:T(8,128)S(1)} %get-tuple-element.17.own_ref), channel_id=1, source_target_pairs={{4,0},{8,4},{12,8},{16,12},{20,16},{24,20},{28,24},{32,28},{36,32}... | collective-permute-start | bytes 245768 | tf_op jit(solution)/shard_map/ppermute | solution.py:604
  52.2 2.1 %collective-permute-start.2 = (f32[160,128]{1,0:T(8,128)S(1)}, f32[160,128]{1,0:T(8,128)S(1)}, u32[]{:S(2)}, u32[]{:S(2)}) collective-permute-start(f32[160,128]{1,0:T(8,128)S(1)} %get-tuple-element.17.own_ref), channel_id=1, source_target_pairs={{0,4},{4,8},{8,12},{12,16},{16,20},{20,24},{24,28},{28,32},{32,36}... | collective-permute-start | bytes 245768 | tf_op jit(solution)/shard_map/ppermute | solution.py:604
  54.3 0.7 copy.17.far_any
  55.0 17.3 %shard_map.156 = (f32[16,2048]{1,0:T(8,128)S(1)}, f32[16,2048]{1,0:T(8,128)S(1)}) custom-call(s32[5]{0:T(128)S(1)} %stack.23.base, f32[40,2048]{1,0:T(8,128)} %copy-done.4, f32[40,2048]{1,0:T(8,128)} %copy-done.1, f32[40,2048]{1,0:T(8,128)} %copy-done, s32[32,27]{1,0:T(8,128)} %near_any.1, s32[32,24]{1,0:T(8,128)} %copy.17.far_any), custom_call_target="tpu_custom_call" | custom-call | flops 140000000 | bytes 4194304 | tf_op jit(solution)/shard_map/pallas_call | solution.py:584
  72.3 3.2 %shard_map.157 = (f32[32,128]{1,0:T(8,128)S(1)}, s32[16,128]{1,0:T(8,128)S(1)}) custom-call(s32[5]{0:T(128)S(1)} %stack.23.base, f32[16,2048]{1,0:T(8,128)S(1)} %get-tuple-element.16.near_any.near_ref, s32[16,16]{1,0:T(8,128)} %cluster_any.4, s32[1,2048]{1,0:T(1,128)} %order_any.3, f32[160,128]{1,0:T(8,128)S(1)} %get-tuple-element.17.own_ref, ...), custom_call_target="tpu_custom_call" | custom-call | flops 5242880 | bytes 4194304 | tf_op jit(solution)/shard_map/pallas_call | solution.py:584
  75.5 8.8 %shard_map.158 = f32[8,64,128]{2,1,0:T(8,128)S(1)} custom-call(s32[5]{0:T(128)S(1)} %stack.23.base, s32[512]{0:T(512)} %counts_any.1, s32[512,128]{1,0:T(8,128)} %table_any.1, f32[64,1,1280]{2,1,0:T(1,128)S(1)} %all-to-all-done.1.source_ref, f32[32,128]{1,0:T(8,128)S(1)} %get-tuple-element.18.z1_ref, f32[160,128]{1,0:T(8,128)S(1)} %get-tuple-element.17.own_ref, ...), custom_call_target="tpu_custom_call" | custom-call | bytes 4194304 | tf_op jit(solution)/shard_map/pallas_call | solution.py:584
  84.3 8.6 %all_to_all.16.group_ref = f32[8,64,128]{2,1,0:T(8,128)S(1)} all-to-all(f32[8,64,128]{2,1,0:T(8,128)S(1)} %shard_map.158), channel_id=1, replica_groups=mesh['yh'=2,'z'=16,'xh'=2,'xl'=2,'sub'=4] {'xl','sub'}, dimensions={0} | all-to-all | bytes 524288 | tf_op jit(solution)/shard_map/all_to_all | solution.py:715
  92.9 3.8 %shard_map.159 = f32[16,2048]{1,0:T(8,128)} custom-call(s32[5]{0:T(128)S(1)} %stack.23.base, s32[32]{0:T(128)} %leaf_any.3, s32[16]{0:T(128)} %cluster_any.5, f32[8,64,128]{2,1,0:T(8,128)S(1)} %all_to_all.16.group_ref, f32[16,2048]{1,0:T(8,128)S(1)} %get-tuple-element.16.near_any.near_ref, f32[16,2048]{1,0:T(8,128)S(1)} %get-tuple-element.19.far_ref, ...), custom_call_target="tpu_custom_call" | custom-call | bytes 4194304 | tf_op jit(solution)/shard_map/pallas_call | solution.py:584
  (15 shorter events, 0.0 us)
Async XLA Ops:
  0.0 1.2 %copy-start.5 = (f32[32,4096]{1,0:T(8,128)S(1)}, f32[32,4096]{1,0:T(8,128)}, u32[]{:S(2)}) copy-start(f32[32,4096]{1,0:T(8,128)} %param.19) | copy-start | bytes 1572868
  1.2 1.0 %copy-start.6 = (f32[32,4096]{1,0:T(8,128)S(1)}, f32[32,4096]{1,0:T(8,128)}, u32[]{:S(2)}) copy-start(f32[32,4096]{1,0:T(8,128)} %param.23) | copy-start | bytes 1572868
  5.9 23.9 %copy-start.4 = (f32[40,2048]{1,0:T(8,128)}, f32[40,2048]{1,0:T(8,128)S(1)}, u32[]{:S(2)}) copy-start(f32[40,2048]{1,0:T(8,128)S(1)} %get-tuple-element.13.own_any) | copy-start | bytes 983044
  5.9 22.5 %collective-permute-start.1 = (f32[40,2048]{1,0:T(8,128)S(1)}, f32[40,2048]{1,0:T(8,128)S(1)}, u32[]{:S(2)}, u32[]{:S(2)}) collective-permute-start(f32[40,2048]{1,0:T(8,128)S(1)} %get-tuple-element.13.own_any), channel_id=1, source_target_pairs={{1,0},{2,1},{3,2},{4,3},{5,4},{6,5},{7,6},{8,7},{9,8},{10,9},{11,1... | collective-permute-start | bytes 983048 | tf_op jit(solution)/shard_map/ppermute | solution.py:598
  8.0 20.4 %collective-permute-start = (f32[40,2048]{1,0:T(8,128)S(1)}, f32[40,2048]{1,0:T(8,128)S(1)}, u32[]{:S(2)}, u32[]{:S(2)}) collective-permute-start(f32[40,2048]{1,0:T(8,128)S(1)} %get-tuple-element.13.own_any), channel_id=1, source_target_pairs={{0,1},{1,2},{2,3},{3,4},{4,5},{5,6},{6,7},{7,8},{8,9},{9,10},{10,1... | collective-permute-start | bytes 983048 | tf_op jit(solution)/shard_map/ppermute | solution.py:598
  10.3 18.2 %copy-start.2 = (f32[16,192]{1,0:T(8,128)S(1)}, f32[16,192]{1,0:T(8,128)}, u32[]{:S(2)}) copy-start(f32[16,192]{1,0:T(8,128)} %cluster_skel_ref.1) | copy-start | bytes 36868
  10.3 18.2 %copy-start.3 = (f32[4,192]{1,0:T(4,128)S(1)}, f32[4,192]{1,0:T(4,128)}, u32[]{:S(2)}) copy-start(f32[4,192]{1,0:T(4,128)} %top_skel_ref.1) | copy-start | bytes 9220
  28.4 1.4 %copy-start = (f32[40,2048]{1,0:T(8,128)}, f32[40,2048]{1,0:T(8,128)S(1)}, u32[]{:S(2)}) copy-start(f32[40,2048]{1,0:T(8,128)S(1)} %collective-permute-done.1.after_any) | copy-start | bytes 983044
  28.5 1.3 %copy-start.1 = (f32[40,2048]{1,0:T(8,128)}, f32[40,2048]{1,0:T(8,128)S(1)}, u32[]{:S(2)}) copy-start(f32[40,2048]{1,0:T(8,128)S(1)} %collective-permute-done.before_any) | copy-start | bytes 983044
  29.8 24.5 %copy-start.7 = (s32[32,24]{0,1:T(8,128)S(1)}, s32[32,24]{0,1:T(8,128)}, u32[]{:S(2)}) copy-start(s32[32,24]{0,1:T(8,128)} %param.21) | copy-start | bytes 9220
  29.8 45.7 %all-to-all-start.1 = ((f32[64,1,1280]{2,1,0:T(1,128)}), f32[64,1,1280]{2,1,0:T(1,128)S(1)}, u32[]{:S(2)}, u32[]{:S(2)}) async-start(f32[64,1,1280]{2,1,0:T(1,128)} %get-tuple-element.15), calls=%async_computation.1 | async-start | bytes 655360 | tf_op jit(solution)/shard_map/all_to_all | solution.py:653
  44.2 28.0 %collective-permute-start.3 = (f32[160,128]{1,0:T(8,128)S(1)}, f32[160,128]{1,0:T(8,128)S(1)}, u32[]{:S(2)}, u32[]{:S(2)}) collective-permute-start(f32[160,128]{1,0:T(8,128)S(1)} %get-tuple-element.17.own_ref), channel_id=1, source_target_pairs={{4,0},{8,4},{12,8},{16,12},{20,16},{24,20},{28,24},{32,28},{36,32}... | collective-permute-start | bytes 245768 | tf_op jit(solution)/shard_map/ppermute | solution.py:604
  52.2 20.1 %collective-permute-start.2 = (f32[160,128]{1,0:T(8,128)S(1)}, f32[160,128]{1,0:T(8,128)S(1)}, u32[]{:S(2)}, u32[]{:S(2)}) collective-permute-start(f32[160,128]{1,0:T(8,128)S(1)} %get-tuple-element.17.own_ref), channel_id=1, source_target_pairs={{0,4},{4,8},{8,12},{12,16},{16,20},{20,24},{24,28},{28,32},{32,36}... | collective-permute-start | bytes 245768 | tf_op jit(solution)/shard_map/ppermute | solution.py:604
